TPU v7x, 256 devices: a whole 4x4x8 slice. The times are simulated.
256 devices in a mesh: ckpt: 8 (over y_hi, x), fsdp: 32 (over z, y_lo, core).
Axes of the slice: x: 4, y: 4 (y_hi: 2, y_lo: 2; y = y_hi * 2 + y_lo), z: 8, core: 2. Of those that a mesh axis runs over, the one named last changes fastest.
Arguments:
- states: bfloat16 [8, 16384, 768], P('ckpt', 'fsdp'), may hold values from -420 to 420
- state_tangent: bfloat16 [8, 16384, 768], P('ckpt', 'fsdp'), may hold values from -12 to 12
- loss_grad: bfloat16 [8, 16384, 768], P('ckpt', 'fsdp'), may hold values from -0.21875 to 0.21875
- norm_gain: bfloat16 [8, 768], P('ckpt'), may hold values from 0.099609375 to 1.8984375
- gain_costate: bfloat16 [8, 768], P('ckpt'), may hold values from -3 to 3
- qkv_weight: bfloat16 [8, 2304, 768], P('ckpt', 'fsdp'), may hold values from -3.1 to 3.1
- qkv_costate: bfloat16 [8, 2304, 768], P('ckpt', 'fsdp'), may hold values from -0.21875 to 0.21875
- out_weight: bfloat16 [8, 768, 768], P('ckpt', 'fsdp'), may hold values from -0.21875 to 0.21875
- out_costate: bfloat16 [8, 768, 768], P('ckpt', 'fsdp'), may hold values from -0.21875 to 0.21875
Outputs:
- scores: float32 [16384], P('fsdp')
All inputs are finite; a program needn't handle non-finite values.
Results may differ from a plain program's by a relative error of at most 0.006.
The roundings to bfloat16 on the way count: a program that leaves them out, or rounds other values in their place, can miss the bound.
Values may be sent and summed in bfloat16 or wider, within the bound.
A program may use at most 64 MiB of HBM per device.

v0:
```python
import math

import jax
import jax.numpy as jnp
from jax import lax
from jax.sharding import PartitionSpec as P

HEADS = 12
HEAD_DIM = 64
SEQ = 512


EPSILON = 1e-05
NEGATIVE = -1e30


def normalize(hidden, hidden_tangent, gain_vector, gain_tangent):
    widened = hidden.astype(jnp.float32)
    widened_tangent = hidden_tangent.astype(jnp.float32)
    inverse_rms = lax.rsqrt(jnp.mean(widened * widened, axis=1, keepdims=True) + EPSILON)
    normed = widened * inverse_rms
    cross_mean = jnp.mean(widened * widened_tangent, axis=1, keepdims=True)
    normed_tangent = (
        widened_tangent * inverse_rms
        - widened * (inverse_rms * inverse_rms * inverse_rms) * cross_mean
    )
    gain_wide = gain_vector.astype(jnp.float32)
    lifted = (gain_wide * normed).astype(jnp.bfloat16)
    lifted_tangent = (
        gain_tangent.astype(jnp.float32) * normed + gain_wide * normed_tangent
    ).astype(jnp.bfloat16)
    return (lifted, lifted_tangent)


def dot_rows(left_side, right_side):
    return lax.dot_general(
        left_side, right_side, (((1,), (1,)), ((), ())), preferred_element_type=jnp.float32
    )


def project_pair(lifted, lifted_tangent, weight_pair):
    primal = dot_rows(lifted, weight_pair[0])
    tangent = dot_rows(lifted_tangent, weight_pair[0]) + dot_rows(lifted, weight_pair[1])
    return jnp.stack((primal, tangent), axis=0)


def output_terms(attended, attended_tangent, weight_pair):
    return dot_rows(attended_tangent, weight_pair[0]) + dot_rows(attended, weight_pair[1])


def attend(primal, tangent, batch_count):
    model_width = primal.shape[1] // 3
    score_multiplier = 1.0 / math.sqrt(HEAD_DIM)

    def split_heads(block):
        return block.reshape(batch_count, SEQ, HEADS, HEAD_DIM).transpose(2, 0, 1, 3)

    row_index = lax.broadcasted_iota(jnp.int32, (SEQ, SEQ), 0)
    col_index = lax.broadcasted_iota(jnp.int32, (SEQ, SEQ), 1)
    causal = row_index >= col_index

    def one_head(operands):
        (
            query_head_slice,
            key_head_slice,
            value_head_slice,
            query_direction,
            key_direction,
            value_direction,
        ) = operands
        attention_logits = (
            jnp.einsum(
                "urs,ups->urp", query_head_slice, key_head_slice, preferred_element_type=jnp.float32
            )
            * score_multiplier
        )
        attention_logits = jnp.where(causal, attention_logits, NEGATIVE)
        row_max = jnp.max(attention_logits, axis=-1, keepdims=True)
        exponent = jnp.exp(attention_logits - row_max)
        attention = exponent / jnp.sum(exponent, axis=-1, keepdims=True)
        logit_derivative = (
            jnp.einsum(
                "urs,ups->urp", query_direction, key_head_slice, preferred_element_type=jnp.float32
            )
            + jnp.einsum(
                "urs,ups->urp", query_head_slice, key_direction, preferred_element_type=jnp.float32
            )
        ) * score_multiplier
        attention_tangent = attention * (
            logit_derivative - jnp.sum(attention * logit_derivative, axis=-1, keepdims=True)
        )
        lowered_precision_weights = attention.astype(jnp.bfloat16)
        lowered_precision_tangent = attention_tangent.astype(jnp.bfloat16)
        block_output = jnp.einsum(
            "eyo,eom->eym",
            lowered_precision_weights,
            value_head_slice,
            preferred_element_type=jnp.float32,
        )
        output_derivative = jnp.einsum(
            "eyo,eom->eym",
            lowered_precision_tangent,
            value_head_slice,
            preferred_element_type=jnp.float32,
        ) + jnp.einsum(
            "eyo,eom->eym",
            lowered_precision_weights,
            value_direction,
            preferred_element_type=jnp.float32,
        )
        return (block_output.astype(jnp.bfloat16), output_derivative.astype(jnp.bfloat16))

    operands = (
        split_heads(primal[:, :model_width]),
        split_heads(primal[:, model_width : 2 * model_width]),
        split_heads(primal[:, 2 * model_width :]),
        split_heads(tangent[:, :model_width]),
        split_heads(tangent[:, model_width : 2 * model_width]),
        split_heads(tangent[:, 2 * model_width :]),
    )
    attended, attended_tangent = lax.map(one_head, operands)

    def merge_heads(block):
        return block.transpose(1, 2, 0, 3).reshape(batch_count * SEQ, HEADS * HEAD_DIM)

    return (merge_heads(attended), merge_heads(attended_tangent))


def per_device(
    states,
    state_tangent,
    loss_grad,
    norm_gain,
    gain_costate,
    qkv_weight,
    qkv_costate,
    out_weight,
    out_costate,
):
    hidden = states[0]
    hidden_tangent = state_tangent[0]
    gradient = loss_grad[0]
    batch_count = hidden.shape[0] // SEQ
    lifted, lifted_tangent = normalize(hidden, hidden_tangent, norm_gain[0], gain_costate[0])
    qkv_pair = jnp.stack((qkv_weight[0], qkv_costate[0]), axis=0)
    out_pair = jnp.stack((out_weight[0], out_costate[0]), axis=0)
    projected = project_pair(
        lifted, lifted_tangent, lax.all_gather(qkv_pair, "fsdp", axis=1, tiled=True)
    )
    rounded = projected.astype(jnp.bfloat16)
    attended, attended_tangent = attend(rounded[0], rounded[1], batch_count)
    residual_term = jnp.sum(
        gradient.astype(jnp.float32) * hidden_tangent.astype(jnp.float32), axis=1
    )
    partial_out = output_terms(
        attended, attended_tangent, lax.all_gather(out_pair, "fsdp", axis=1, tiled=True)
    )
    token_score = residual_term + jnp.sum(gradient.astype(jnp.float32) * partial_out, axis=1)
    return lax.psum(token_score, "ckpt")


def solution(mesh):
    return jax.shard_map(
        per_device,
        mesh=mesh,
        in_specs=(
            P("ckpt", "fsdp", None),
            P("ckpt", "fsdp", None),
            P("ckpt", "fsdp", None),
            P("ckpt", None),
            P("ckpt", None),
            P("ckpt", "fsdp", None),
            P("ckpt", "fsdp", None),
            P("ckpt", "fsdp", None),
            P("ckpt", "fsdp", None),
        ),
        out_specs=P("fsdp"),
        check_vma=False,
    )
```

profile of v0, /device:TPU:1, one launch (start us, length us, event | category | flops | bytes accessed | tf_op | source)
XLA Modules:
  0.0 216.3 jit_solution(2809314633785675304)
XLA Ops:
  6.6 1.8 pad_maximum_fusion
  9.9 2.3 %fusion.57 = (f32[512]{0:T(512)S(1)}, f32[512]{0:T(512)S(1)}, f32[512]{0:T(512)S(1)}) fusion(bf16[1,512,768]{2,1,0:T(8,128)(2,1)} %param.12, bf16[1,512,768]{2,1,0:T(8,128)(2,1)} %param.11, bf16[1,512,768]{2,1,0:T(8,128)(2,1)} %param.13), kind=kLoop, calls=%fused_computation.72 | loop fusion | flops 3537408 | bytes 2365440 | tf_op jit(solution)/shard_map/reduce_sum | solution.py:22
  12.2 72.2 %all-gather.3.cloned.1.call-done = bf16[2,2304,768]{2,1,0:T(8,128)(2,1)} async-done(((bf16[2,72,768]{2,1,0:T(8,128)(2,1)}), bf16[2,2304,768]{2,1,0:T(8,128)(2,1)}) %all-gather.3.cloned.1.call-update) | async-done | bytes 7077904 | tf_op jit(solution)/shard_map/all_gather | solution.py:148
  84.4 4.6 %fusion.44 = f32[512,2304]{1,0:T(8,128)S(1)} fusion(bf16[2,2304,768]{2,1,0:T(8,128)(2,1)} %all-gather.3.cloned.1.call-done, bf16[1,512,768]{2,1,0:T(8,128)(2,1)S(1)} %copy-done, bf16[1,512,768]{2,1,0:T(8,128)(2,1)S(1)} %copy-done.1, f32[512]{0:T(512)S(1)} %get-tuple-element.122, f32[512]{0:T(512)S(1)} %get-tuple-element.120, ...), kind=kOutput, calls=%fused_computation.52 | convolution fusion | flops 1816264704 | bytes 9842688 | tf_op jit(solution)/shard_map/dot_general | solution.py:36
  89.1 2.1 fusion.43
  94.1 4.1 %convolution_convert_fusion.1 = bf16[512,2304]{1,0:T(8,128)(2,1)S(1)} fusion(bf16[2,2304,768]{2,1,0:T(8,128)(2,1)} %all-gather.3.cloned.1.call-done, bf16[1,512,768]{2,1,0:T(8,128)(2,1)S(1)} %copy-done.2, f32[512]{0:T(512)S(1)} %get-tuple-element.121, f32[768]{0:T(1024)S(1)} %get-tuple-element.124), kind=kOutput, calls=%fused_computation.49 | convolution fusion | flops 1814691840 | bytes 6689792 | tf_op jit(solution)/shard_map/dot_general | solution.py:36
  100.1 83.9 %while.13 = (s32[]{:T(128)}, bf16[12,1,512,64]{2,3,1,0:T(8,128)(2,1)}, bf16[12,1,512,64]{2,3,1,0:T(8,128)(2,1)}, bf16[12,1,512,64]{2,3,0,1:T(8,128)(2,1)S(1)}, b...) while((s32[]{:T(128)}, ...), condition=%wide.region_7.8_spmd.clone, body=%wide.region_3.7_spmd.clone.sunk | while | flops 207452672 | bytes 11501157 | solution.py:121
  103.5 1.8 fusion.100
  105.3 1.8 fusion.97
  110.5 1.8 fusion.100
  112.3 1.8 fusion.97
  117.5 1.8 fusion.100
  119.3 1.8 fusion.97
  124.5 1.8 fusion.100
  126.3 1.8 fusion.97
  131.5 1.8 fusion.100
  133.2 1.8 fusion.97
  138.5 1.8 fusion.100
  140.2 1.8 fusion.97
  145.4 1.8 fusion.100
  147.2 1.8 fusion.97
  152.4 1.8 fusion.100
  159.4 1.8 fusion.100
  161.2 1.8 fusion.97
  166.4 1.8 fusion.100
  168.2 1.8 fusion.97
  173.4 1.8 fusion.100
  180.4 1.8 fusion.100
  182.2 1.8 fusion.97
  183.9 2.5 %fusion.59 = f32[512,768]{1,0:T(8,128)S(1)} fusion(bf16[512,768]{0,1:T(8,128)(2,1)} %bitcast.148, bf16[2,768,768]{2,1,0:T(8,128)(2,1)} %all-gather.5.cloned.1.call-done), kind=kOutput, calls=%fused_computation.76 | convolution fusion | flops 603979776 | bytes 3538944 | tf_op jit(solution)/shard_map/dot_general | solution.py:36
  186.4 2.1 fusion.55
  188.5 20.9 %psum.7 = f32[512]{0:T(512)} all-reduce(f32[512]{0:T(512)S(1)} %add.45), channel_id=1, replica_groups=mesh['ckpt'=8,'fsdp'=32] {'ckpt'}, use_global_device_ids=true, to_apply=%region_9.10 | all-reduce | flops 512 | bytes 4096 | tf_op jit(solution)/shard_map/psum | solution.py:159
  (97 shorter events, 51.1 us)
Async XLA Ops:
  6.5 77.9 %copy-start.1 = (bf16[1,512,768]{2,1,0:T(8,128)(2,1)S(1)}, bf16[1,512,768]{2,1,0:T(8,128)(2,1)}, u32[]{:S(2)}) copy-start(bf16[1,512,768]{2,1,0:T(8,128)(2,1)} %param.11) | copy-start | bytes 2359300
  6.5 77.9 %copy-start = (bf16[1,512,768]{2,1,0:T(8,128)(2,1)S(1)}, bf16[1,512,768]{2,1,0:T(8,128)(2,1)}, u32[]{:S(2)}) copy-start(bf16[1,512,768]{2,1,0:T(8,128)(2,1)} %param.12) | copy-start | bytes 2359300
  6.5 5.6 %copy-start.5 = (bf16[1,768]{1,0:T(2,128)(2,1)S(1)}, bf16[1,768]{1,0:T(2,128)(2,1)}, u32[]{:S(2)}) copy-start(bf16[1,768]{1,0:T(2,128)(2,1)} %param.14) | copy-start | bytes 4612
  6.5 5.7 %copy-start.4 = (bf16[1,768]{1,0:T(2,128)(2,1)S(1)}, bf16[1,768]{1,0:T(2,128)(2,1)}, u32[]{:S(2)}) copy-start(bf16[1,768]{1,0:T(2,128)(2,1)} %param.15) | copy-start | bytes 4612
  6.5 77.9 %all-gather.3.cloned.1.call-start = ((), (), s32[]{:S(2)}) async-start(), calls=%async_computation | async-start | bytes 7299072 | tf_op jit(solution)/shard_map/all_gather | solution.py:148
  8.4 175.5 %all-gather.5.cloned.1.call-start = ((), (), s32[]{:S(2)}) async-start(), calls=%async_computation.1 | async-start | bytes 2433024 | tf_op jit(solution)/shard_map/all_gather | solution.py:156
  84.4 4.6 %copy-start.6 = (bf16[2,2304,768]{2,1,0:T(8,128)(2,1)S(1)}, bf16[2,2304,768]{2,1,0:T(8,128)(2,1)}, u32[]{:S(2)}) copy-start(bf16[2,2304,768]{2,1,0:T(8,128)(2,1)} %all-gather.3.cloned.1.call-done) | copy-start | bytes 21233668
  91.7 2.4 %copy-start.2 = (bf16[1,512,768]{2,1,0:T(8,128)(2,1)S(1)}, bf16[1,512,768]{2,1,0:T(8,128)(2,1)}, u32[]{:S(2)}) copy-start(bf16[1,512,768]{2,1,0:T(8,128)(2,1)} %param.11) | copy-start | bytes 2359300
  183.9 2.5 %copy-start.3 = (bf16[1,512,768]{2,1,0:T(8,128)(2,1)S(1)}, bf16[1,512,768]{2,1,0:T(8,128)(2,1)}, u32[]{:S(2)}) copy-start(bf16[1,512,768]{2,1,0:T(8,128)(2,1)} %param.13) | copy-start | bytes 2359300
  183.9 2.5 %copy-start.7 = (bf16[2,768,768]{2,1,0:T(8,128)(2,1)S(1)}, bf16[2,768,768]{2,1,0:T(8,128)(2,1)}, u32[]{:S(2)}) copy-start(bf16[2,768,768]{2,1,0:T(8,128)(2,1)} %all-gather.5.cloned.1.call-done) | copy-start | bytes 7077892
Sparse Core Ops, SparseCore 0:
  9.2 75.2 all-gather.2
  86.2 65.2 all-gather.4
where the time goes:
time: 220 us; the launch traced here: 216 us
  matrix products  96.8 us (44%)
  waiting for transfers between devices  72.2 us (33%)
  blocking collectives  20.9 us (10%)
  between operations  13.5 us (6%)
  other arithmetic  7.9 us (4%)
  local copies, waits for them, and re-layouts  4.71 us (2%)
    all_gather x1, waiting for transfers between devices, per_device(): lax.all_gather(qkv_pair, 'fsdp', axis=1, tiled=True)  72.2 us
    dot_general x12, matrix products, one_head(): jnp.einsum('eyo,eom->eym', lowered_precision_weights, value_direction, pr...  21.3 us
    dot_general x12, matrix products, one_head(): jnp.einsum('eyo,eom->eym', lowered_precision_weights, value_head_slice, p...  21.2 us
    psum x1, blocking collectives, per_device(): return lax.psum(token_score, 'ckpt')  20.9 us
    dot_general x12, matrix products, one_head(): jnp.einsum('urs,ups->urp', query_head_slice, key_direction, preferred_ele...  15.5 us
    dot_general x5, matrix products, dot_rows(): lax.dot_general(left_side, right_side, (((1,), (1,)), ((), ())), preferre...  15.4 us
    dot_general x12, matrix products, one_head(): jnp.einsum('eyo,eom->eym', lowered_precision_tangent, value_head_slice, p...  14.9 us
  transfers between devices with their start and end apart: 2, of which 1 were waited for; matrix products, arithmetic and copies ran while one was open for 48% of the time, Pallas kernels for 0%

commit v1 on v0

v1 whole, which is shorter than its diff:
```python
import functools
import math

import jax
import jax.numpy as jnp
from jax import lax
from jax.experimental import pallas as pl
from jax.experimental.pallas import tpu as pltpu
from jax.sharding import PartitionSpec as P

D = 768
HEADS = 12
HD = 64
SEQ = 512
EPSILON = 1e-05
NEGATIVE = -1e30
BF16 = jnp.bfloat16
F32 = jnp.float32
MESH = pl.DeviceIdType.MESH
NZ = 8
NCKPT = 8
NDEV = 32
RQ = 144
RO = 48

PIECES = (
    (("B", 64, 80, (64, 48), (112, 32)), ("A", 0, 64, (0, 32), (32, 32)), ("X", 0, 64, (0, 32), (32, 32))),
    (("B", 16, 32, (16, 16), (32, 16)), ("A", 0, 16, (0, 16), None), ("X", 0, 16, None, (0, 16))),
)


def dot(a, b):
    return lax.dot_general(a, b, (((1,), (0,)), ((), ())), preferred_element_type=F32)


def normalize(x_ref, t_ref, g_ref, gain_ref, cost_ref, lt_ref, ltt_ref, gt_ref, res_ref):
    gain = gain_ref[...].astype(F32)
    cost = cost_ref[...].astype(F32)

    def body(i, carry):
        rows = pl.ds(pl.multiple_of(i * 128, 128), 128)
        x = x_ref[rows, :].astype(F32)
        t = t_ref[rows, :].astype(F32)
        g = g_ref[rows, :].astype(F32)
        inv = lax.rsqrt(jnp.mean(x * x, axis=1, keepdims=True) + EPSILON)
        normed = x * inv
        cross = jnp.mean(x * t, axis=1, keepdims=True)
        normed_t = t * inv - x * (inv * inv * inv) * cross
        lifted = (gain * normed).astype(BF16)
        lifted_t = (cost * normed + gain * normed_t).astype(BF16)
        lt_ref[:, rows] = lifted.T
        ltt_ref[:, rows] = lifted_t.T
        gt_ref[:, rows] = g.T
        p = g * t
        q = p[:, 0:128]
        for k in range(1, D // 128):
            q = q + p[:, 128 * k : 128 * k + 128]
        res_ref[:, rows] = jnp.sum(q.T, axis=0, keepdims=True)
        return carry

    lax.fori_loop(0, SEQ // 128, body, 0)


def project(zc, gq_ref, lt_ref, ltt_ref, p_ref, dp_ref):
    devs = pl.ds(zc * 4, 4)
    r1 = dot(gq_ref[devs].reshape(4 * RQ, D), lt_ref[...]).reshape(4, RQ, SEQ)
    r2 = dot(gq_ref[devs, 0:80, :].reshape(320, D), ltt_ref[...]).reshape(4, 80, SEQ)
    rows = pl.ds(pl.multiple_of(zc * 288, 288), 288)
    p_ref[rows, :] = r1[:, 0:72].reshape(288, SEQ).astype(BF16)
    dp_ref[rows, :] = (r2[:, 0:72] + r1[:, 72:144]).reshape(288, SEQ).astype(BF16)


def attend_head(h, p_ref, dp_ref, at_ref, dat_ref):
    def rows(base):
        return pl.ds(pl.multiple_of(base + h * HD, HD), HD)

    q, dq = p_ref[rows(0), :], dp_ref[rows(0), :]
    k, dk = p_ref[rows(D), :], dp_ref[rows(D), :]
    v, dv = p_ref[rows(2 * D), :], dp_ref[rows(2 * D), :]
    kd = jnp.concatenate([k, dk], axis=0).T
    rhs_s = jnp.concatenate([q, jnp.zeros_like(q)], axis=0)
    rhs_d = jnp.concatenate([dq, q], axis=0)
    vv = jnp.concatenate([v, dv], axis=0)
    scale2 = math.log2(math.e) / math.sqrt(HD)
    for b in range(2):
        cols = slice(256 * b, 256 * b + 256)
        jm = 256 * (b + 1)
        s = dot(kd[:jm], rhs_s[:, cols])
        d = dot(kd[:jm], rhs_d[:, cols])
        row = lax.broadcasted_iota(jnp.int32, (256, 256), 0)
        col = lax.broadcasted_iota(jnp.int32, (256, 256), 1)
        diag = jnp.where(row <= col, s[jm - 256 :], NEGATIVE)
        s = diag if b == 0 else jnp.concatenate([s[: jm - 256], diag], axis=0)
        m = jnp.max(s, axis=0, keepdims=True)
        e = jnp.exp2((s - m) * scale2)
        r = 1.0 / jnp.sum(e, axis=0, keepdims=True)
        t = jnp.sum(e * d, axis=0, keepdims=True) * r
        a = (e * r).astype(BF16)
        da = ((e * (r * (1.0 / math.sqrt(HD)))) * (d - t)).astype(BF16)
        o1 = dot(vv[:, :jm], a)
        o2 = dot(v[:, :jm], da)
        at_ref[rows(0), cols] = o1[:HD].astype(BF16)
        dat_ref[rows(0), cols] = (o1[HD:] + o2).astype(BF16)


def out_scores(go_ref, at_ref, dat_ref, gt_ref):
    total = jnp.zeros((1, SEQ), F32)
    for b in range(2):
        devs = slice(16 * b, 16 * b + 16)
        r1 = dot(go_ref[devs, 0:32, :].reshape(512, D), dat_ref[...]).reshape(16, 32, SEQ)
        r2 = dot(go_ref[devs, 16:48, :].reshape(512, D), at_ref[...]).reshape(16, 32, SEQ)
        po = (r1[:, 0:24] + r2[:, 8:32]).reshape(384, SEQ)
        total = total + jnp.sum(po * gt_ref[384 * b : 384 * b + 384, :], axis=0, keepdims=True)
    return total


def kernel(
    x_hbm, t_hbm, g_hbm, gain_ref, cost_ref, wq_hbm, cq_hbm, wo_hbm, co_hbm,
    out_ref,
    x_ref, t_ref, g_ref, wq_ref, cq_ref, wo_ref, co_ref,
    gq_ref, go_ref, lt_ref, ltt_ref, gt_ref, res_ref, p_ref, dp_ref, at_ref, dat_ref,
    mine_ref, sums_ref,
    in_sem, ring_s, ring_r, y_s, y_r, sib_s, sib_r, sum_s, sum_r,
):
    ck = lax.axis_index("ckpt")
    me = lax.axis_index("fsdp")
    z = me // 4
    y = (me // 2) % 2
    c = me % 2

    def dev(zz, yy, cc):
        return zz * 4 + yy * 2 + cc

    def zrel(r):
        return (z + (r + NZ)) % NZ

    up = dev(zrel(1), y, c)
    down = dev(zrel(-1), y, c)
    side = dev(z, 1 - y, c)
    twin = dev(z, y, 1 - c)

    loads = [
        pltpu.make_async_copy(src, dst, in_sem.at[i])
        for i, (src, dst) in enumerate(
            (
                (wq_hbm.at[0], wq_ref), (cq_hbm.at[0], cq_ref), (wo_hbm.at[0], wo_ref), (co_hbm.at[0], co_ref),
                (x_hbm.at[0], x_ref), (t_hbm.at[0], t_ref), (g_hbm.at[0], g_ref),
            )
        )
    ]
    for load in loads:
        load.start()

    barrier = pltpu.get_barrier_semaphore()
    for peer in (up, down, side, twin):
        pl.semaphore_signal(barrier, inc=1, device_id={"fsdp": peer}, device_id_type=MESH)
    for k in range(1, NCKPT):
        pl.semaphore_signal(barrier, inc=1, device_id={"ckpt": (ck + k) % NCKPT}, device_id_type=MESH)

    bufs = (gq_ref, go_ref)
    pending = []

    def send(src, dst, ssem, rsem, peer):
        copy = pltpu.make_async_remote_copy(
            src_ref=src, dst_ref=dst, send_sem=ssem, recv_sem=rsem, device_id={"fsdp": peer}, device_id_type=MESH
        )
        copy.start()
        pending.append(copy)

    def landed(ref, sem):
        pltpu.make_async_copy(ref, ref, sem).wait()

    def part(ph, r, yy, cc, first, count):
        return bufs[ph].at[dev(zrel(r), yy, cc), pl.ds(first, count), :]

    def whole(ph, r, yy, cc):
        return bufs[ph].at[dev(zrel(r), yy, cc)]

    def owner_y(kind):
        return 1 - y if kind == "X" else y

    def hop_rows(piece, way, s):
        kind, first, count, last_up, last_down = piece
        if s < 3:
            return (first, count)
        return last_up if way == 0 else last_down

    def ring_send(ph, pi, way, s):
        piece = PIECES[ph][pi]
        span = hop_rows(piece, way, s)
        if span is None:
            return
        r = -s if way == 0 else s
        ref = part(ph, r, owner_y(piece[0]), c, *span)
        send(ref, ref, ring_s.at[ph, way, s, pi], ring_r.at[ph, way, s, pi], up if way == 0 else down)

    def ring_wait(ph, pi, way, s):
        piece = PIECES[ph][pi]
        span = hop_rows(piece, way, s)
        if span is None:
            return
        r = -(s + 1) if way == 0 else s + 1
        landed(part(ph, r, owner_y(piece[0]), c, *span), ring_r.at[ph, way, s, pi])

    def y_send(ph, pi, r):
        _, first, count, _, _ = PIECES[ph][pi]
        slot = 8 if pi == 1 else r % NZ
        ref = part(ph, r, y, c, first, count)
        send(ref, ref, y_s.at[ph, slot], y_r.at[ph, slot], side)

    def y_wait(ph, pi, r):
        _, first, count, _, _ = PIECES[ph][pi]
        slot = 8 if pi == 1 else r % NZ
        landed(part(ph, r, 1 - y, c, first, count), y_r.at[ph, slot])

    def twin_send(ph, r, other):
        ref = whole(ph, r, 1 - y if other else y, c)
        send(ref, ref, sib_s.at[ph, r % NZ, other], sib_r.at[ph, r % NZ, other], twin)

    def twin_wait(ph, r):
        for other in (0, 1):
            landed(whole(ph, r, 1 - y if other else y, 1 - c), sib_r.at[ph, r % NZ, other])

    def begin(ph):
        y_send(ph, 1, 0)
        for pi in (0, 1):
            for way in (0, 1):
                ring_send(ph, pi, way, 0)
        y_send(ph, 0, 0)
        twin_send(ph, 0, 0)
        y_wait(ph, 1, 0)
        for way in (0, 1):
            ring_send(ph, 2, way, 0)

    def finish_own(ph):
        y_wait(ph, 0, 0)
        twin_send(ph, 0, 1)

    def hop(ph, s):
        rels = (-(s + 1), s + 1)
        for pi in range(3):
            for way in (0, 1):
                ring_wait(ph, pi, way, s)
                if s < 3:
                    ring_send(ph, pi, way, s + 1)
                    if pi == 0:
                        y_send(ph, 0, rels[way])
                    if pi == 1:
                        twin_send(ph, rels[way], 0)
            if s == 3 and pi == 0:
                y_send(ph, 0, 4)
            if s == 3 and pi == 1:
                twin_send(ph, 4, 0)
        for r in rels if s < 3 else (4,):
            y_wait(ph, 0, r)
            twin_send(ph, r, 1)

    def project_rel(r):
        twin_wait(0, r)
        project(zrel(r), gq_ref, lt_ref, ltt_ref, p_ref, dp_ref)

    for load in loads[:4]:
        load.wait()
    gq_ref[me] = jnp.concatenate([wq_ref[...].astype(F32), cq_ref[...].astype(F32)], axis=0).astype(BF16)
    go_ref[me] = jnp.concatenate([wo_ref[...].astype(F32), co_ref[...].astype(F32)], axis=0).astype(BF16)
    pl.semaphore_wait(barrier, 4 + NCKPT - 1)
    begin(0)

    for load in loads[4:]:
        load.wait()
    normalize(x_ref, t_ref, g_ref, gain_ref, cost_ref, lt_ref, ltt_ref, gt_ref, res_ref)

    finish_own(0)
    hop(0, 0)
    project_rel(0)
    hop(0, 1)
    project_rel(-1)
    project_rel(1)
    hop(0, 2)
    begin(1)
    project_rel(-2)
    project_rel(2)
    hop(0, 3)
    finish_own(1)
    project_rel(-3)
    hop(1, 0)
    project_rel(3)
    project_rel(4)
    for s in range(1, 4):
        hop(1, s)
        lax.fori_loop(
            (s - 1) * 4, s * 4, lambda h, carry: (attend_head(h, p_ref, dp_ref, at_ref, dat_ref), carry)[1], 0
        )
    for r in range(NZ):
        twin_wait(1, r)
    mine_ref[...] = out_scores(go_ref, at_ref, dat_ref, gt_ref) + res_ref[...]

    copies = []
    for k in range(1, NCKPT):
        copy = pltpu.make_async_remote_copy(
            src_ref=mine_ref, dst_ref=sums_ref.at[k], send_sem=sum_s.at[k], recv_sem=sum_r.at[k],
            device_id={"ckpt": (ck + k) % NCKPT}, device_id_type=MESH,
        )
        copy.start()
        copies.append(copy)
    for copy in pending:
        copy.wait_send()
    total = mine_ref[...]
    for k, copy in enumerate(copies):
        copy.wait_recv()
        total = total + sums_ref[k + 1]
    out_ref[...] = total
    for copy in copies:
        copy.wait_send()


def per_device(states, state_tangent, loss_grad, norm_gain, gain_costate, qkv_weight, qkv_costate, out_weight, out_costate):
    anywhere = pl.BlockSpec(memory_space=pl.ANY)
    vmem = pl.BlockSpec(memory_space=pltpu.VMEM)
    out = pl.pallas_call(
        kernel,
        out_shape=jax.ShapeDtypeStruct((1, SEQ), F32),
        in_specs=[anywhere] * 3 + [vmem] * 2 + [anywhere] * 4,
        out_specs=vmem,
        scratch_shapes=[
            pltpu.VMEM((SEQ, D), BF16),
            pltpu.VMEM((SEQ, D), BF16),
            pltpu.VMEM((SEQ, D), BF16),
            pltpu.VMEM((72, D), BF16),
            pltpu.VMEM((72, D), BF16),
            pltpu.VMEM((24, D), BF16),
            pltpu.VMEM((24, D), BF16),
            pltpu.VMEM((NDEV, RQ, D), BF16),
            pltpu.VMEM((NDEV, RO, D), BF16),
            pltpu.VMEM((D, SEQ), BF16),
            pltpu.VMEM((D, SEQ), BF16),
            pltpu.VMEM((D, SEQ), F32),
            pltpu.VMEM((1, SEQ), F32),
            pltpu.VMEM((3 * D, SEQ), BF16),
            pltpu.VMEM((3 * D, SEQ), BF16),
            pltpu.VMEM((D, SEQ), BF16),
            pltpu.VMEM((D, SEQ), BF16),
            pltpu.VMEM((1, SEQ), F32),
            pltpu.VMEM((NCKPT, 1, SEQ), F32),
            pltpu.SemaphoreType.DMA((7,)),
            pltpu.SemaphoreType.DMA((2, 2, 4, 3)),
            pltpu.SemaphoreType.DMA((2, 2, 4, 3)),
            pltpu.SemaphoreType.DMA((2, 9)),
            pltpu.SemaphoreType.DMA((2, 9)),
            pltpu.SemaphoreType.DMA((2, NZ, 2)),
            pltpu.SemaphoreType.DMA((2, NZ, 2)),
            pltpu.SemaphoreType.DMA((NCKPT,)),
            pltpu.SemaphoreType.DMA((NCKPT,)),
        ],
        compiler_params=pltpu.CompilerParams(
            collective_id=0, has_side_effects=True, vmem_limit_bytes=48 * 1024 * 1024
        ),
        cost_estimate=pl.CostEstimate(flops=9_000_000_000, bytes_accessed=3_000_000, transcendentals=3_200_000),
        name="scores",
    )(states, state_tangent, loss_grad, norm_gain, gain_costate, qkv_weight, qkv_costate, out_weight, out_costate)
    return out.reshape(SEQ)


def solution(mesh):
    return jax.shard_map(
        per_device,
        mesh=mesh,
        in_specs=(
            P("ckpt", "fsdp", None),
            P("ckpt", "fsdp", None),
            P("ckpt", "fsdp", None),
            P("ckpt", None),
            P("ckpt", None),
            P("ckpt", "fsdp", None),
            P("ckpt", "fsdp", None),
            P("ckpt", "fsdp", None),
            P("ckpt", "fsdp", None),
        ),
        out_specs=P("fsdp"),
        check_vma=False,
    )
```

time: 220 us -> 90.1 us (0.41)
  the two profiles are of different devices: /device:TPU:1 before, /device:TPU:2 now
where the time goes in v1:
time: 90.1 us; the launch traced here: 89.6 us
  Pallas kernels  80.9 us (90%)
  local copies, waits for them, and re-layouts  8.67 us (10%)
    pallas_call x1, Pallas kernels, per_device(): pl.pallas_call(kernel, out_shape=jax.ShapeDtypeStruct((1, SEQ), F32), in_...  80.9 us
    unnamed x19, local copies, waits for them, and re-layouts  8.67 us

profile of v1, /device:TPU:2, one launch (start us, length us, event | category | flops | bytes accessed | tf_op | source)
XLA Modules:
  0.0 89.6 jit_solution(14259572882984814761)
XLA Ops:
  0.0 0.0 copy-start
  0.0 1.1 %copy-done = bf16[1,512,768]{2,1,0:T(8,128)(2,1)S(1)} copy-done((bf16[1,512,768]{2,1,0:T(8,128)(2,1)S(1)}, bf16[1,512,768]{2,1,0:T(8,128)(2,1)}, u32[]{:S(2)}) %copy-start) | copy-done | bytes 786456
  1.1 0.0 copy-start.1
  1.1 1.1 %copy-done.1 = bf16[1,512,768]{2,1,0:T(8,128)(2,1)S(1)} copy-done((bf16[1,512,768]{2,1,0:T(8,128)(2,1)S(1)}, bf16[1,512,768]{2,1,0:T(8,128)(2,1)}, u32[]{:S(2)}) %copy-start.1) | copy-done | bytes 786456
  2.3 0.0 copy-start.2
  2.3 1.1 %copy-done.2 = bf16[1,512,768]{2,1,0:T(8,128)(2,1)S(1)} copy-done((bf16[1,512,768]{2,1,0:T(8,128)(2,1)S(1)}, bf16[1,512,768]{2,1,0:T(8,128)(2,1)}, u32[]{:S(2)}) %copy-start.2) | copy-done | bytes 786456
  3.4 0.0 copy-start.3
  3.4 0.9 copy-done.3
  4.3 0.0 copy-start.4
  4.3 0.9 copy-done.4
  5.2 0.0 copy-start.5
  5.2 0.8 copy-done.5
  6.0 0.0 copy-start.6
  6.0 0.8 copy-done.6
  6.7 0.0 copy-start.7
  6.7 0.7 copy-done.7
  7.4 0.0 copy-start.8
  7.4 0.7 copy-done.8
  8.1 80.9 %scores.1 = f32[1,512]{1,0:T(1,128)S(1)} custom-call(bf16[1,512,768]{2,1,0:T(8,128)(2,1)S(1)} %copy-done, bf16[1,512,768]{2,1,0:T(8,128)(2,1)S(1)} %copy-done.1, bf16[1,512,768]{2,1,0:T(8,128)(2,1)S(1)} %copy-done.2, bf16[1,768]{1,0:T(2,128)(2,1)S(1)} %copy-done.7, bf16[1,768]{1,0:T(2,128)(2,1)S(1)} %copy-done.8, bf16[1,72,768]{2,1,0:T(8,128)(2,1)S(1)} %copy-done.3, ...), custom_call_target="tpu_custom_call" | custom-call | flops 8999999488 | bytes 3000000 | tf_op jit(solution)/shard_map/scores/pallas_call | solution.py:320
  89.0 0.6 copy.11
Async XLA Ops:
  0.0 1.1 %copy-start = (bf16[1,512,768]{2,1,0:T(8,128)(2,1)S(1)}, bf16[1,512,768]{2,1,0:T(8,128)(2,1)}, u32[]{:S(2)}) copy-start(bf16[1,512,768]{2,1,0:T(8,128)(2,1)} %x_hbm.1) | copy-start | bytes 2359300
  1.1 1.1 %copy-start.1 = (bf16[1,512,768]{2,1,0:T(8,128)(2,1)S(1)}, bf16[1,512,768]{2,1,0:T(8,128)(2,1)}, u32[]{:S(2)}) copy-start(bf16[1,512,768]{2,1,0:T(8,128)(2,1)} %t_hbm.1) | copy-start | bytes 2359300
  2.3 1.1 %copy-start.2 = (bf16[1,512,768]{2,1,0:T(8,128)(2,1)S(1)}, bf16[1,512,768]{2,1,0:T(8,128)(2,1)}, u32[]{:S(2)}) copy-start(bf16[1,512,768]{2,1,0:T(8,128)(2,1)} %g_hbm.1) | copy-start | bytes 2359300
  3.4 0.9 %copy-start.3 = (bf16[1,72,768]{2,1,0:T(8,128)(2,1)S(1)}, bf16[1,72,768]{2,1,0:T(8,128)(2,1)}, u32[]{:S(2)}) copy-start(bf16[1,72,768]{2,1,0:T(8,128)(2,1)} %wq_hbm.1) | copy-start | bytes 331780
  4.3 0.9 %copy-start.4 = (bf16[1,72,768]{2,1,0:T(8,128)(2,1)S(1)}, bf16[1,72,768]{2,1,0:T(8,128)(2,1)}, u32[]{:S(2)}) copy-start(bf16[1,72,768]{2,1,0:T(8,128)(2,1)} %cq_hbm.1) | copy-start | bytes 331780
  5.2 0.8 copy-start.5
  6.0 0.8 copy-start.6
  6.7 0.7 copy-start.7
  7.4 0.7 copy-start.8

commit v2 on v1

--- a/solution.py
+++ b/solution.py
@@ -27,6 +27,18 @@
     (("B", 64, 80, (64, 48), (112, 32)), ("A", 0, 64, (0, 32), (32, 32)), ("X", 0, 64, (0, 32), (32, 32))),
     (("B", 16, 32, (16, 16), (32, 16)), ("A", 0, 16, (0, 16), None), ("X", 0, 16, None, (0, 16))),
 )
+
+
+def remote(src, dst, ssem, rsem, where, tag):
+    copy = pltpu.make_async_remote_copy(
+        src_ref=src, dst_ref=dst, send_sem=ssem, recv_sem=rsem, device_id=where, device_id_type=MESH
+    )
+    copy.start()
+    return copy
+
+
+def landed(ref, sem, tag):
+    pltpu.make_async_copy(ref, ref, sem).wait()
 
 
 def dot(a, b):
@@ -115,9 +127,9 @@
 
 
 def kernel(
-    x_hbm, t_hbm, g_hbm, gain_ref, cost_ref, wq_hbm, cq_hbm, wo_hbm, co_hbm,
+    x_hbm, t_hbm, g_hbm, gain_hbm, cost_hbm, wq_hbm, cq_hbm, wo_hbm, co_hbm,
     out_ref,
-    x_ref, t_ref, g_ref, wq_ref, cq_ref, wo_ref, co_ref,
+    x_ref, t_ref, g_ref, gain_ref, cost_ref, wq_ref, cq_ref, wo_ref, co_ref,
     gq_ref, go_ref, lt_ref, ltt_ref, gt_ref, res_ref, p_ref, dp_ref, at_ref, dat_ref,
     mine_ref, sums_ref,
     in_sem, ring_s, ring_r, y_s, y_r, sib_s, sib_r, sum_s, sum_r,
@@ -144,7 +156,8 @@
         for i, (src, dst) in enumerate(
             (
                 (wq_hbm.at[0], wq_ref), (cq_hbm.at[0], cq_ref), (wo_hbm.at[0], wo_ref), (co_hbm.at[0], co_ref),
-                (x_hbm.at[0], x_ref), (t_hbm.at[0], t_ref), (g_hbm.at[0], g_ref),
+                (x_hbm.at[0], x_ref), (t_hbm.at[0], t_ref), (gain_hbm, gain_ref), (cost_hbm, cost_ref),
+                (g_hbm.at[0], g_ref),
             )
         )
     ]
@@ -160,15 +173,8 @@
     bufs = (gq_ref, go_ref)
     pending = []
 
-    def send(src, dst, ssem, rsem, peer):
-        copy = pltpu.make_async_remote_copy(
-            src_ref=src, dst_ref=dst, send_sem=ssem, recv_sem=rsem, device_id={"fsdp": peer}, device_id_type=MESH
-        )
-        copy.start()
-        pending.append(copy)
-
-    def landed(ref, sem):
-        pltpu.make_async_copy(ref, ref, sem).wait()
+    def send(src, dst, ssem, rsem, peer, tag):
+        pending.append(remote(src, dst, ssem, rsem, {"fsdp": peer}, tag))
 
     def part(ph, r, yy, cc, first, count):
         return bufs[ph].at[dev(zrel(r), yy, cc), pl.ds(first, count), :]
@@ -192,7 +198,7 @@
             return
         r = -s if way == 0 else s
         ref = part(ph, r, owner_y(piece[0]), c, *span)
-        send(ref, ref, ring_s.at[ph, way, s, pi], ring_r.at[ph, way, s, pi], up if way == 0 else down)
+        send(ref, ref, ring_s.at[ph, way, s, pi], ring_r.at[ph, way, s, pi], up if way == 0 else down, ('ring', ph))
 
     def ring_wait(ph, pi, way, s):
         piece = PIECES[ph][pi]
@@ -200,26 +206,30 @@
         if span is None:
             return
         r = -(s + 1) if way == 0 else s + 1
-        landed(part(ph, r, owner_y(piece[0]), c, *span), ring_r.at[ph, way, s, pi])
-
-    def y_send(ph, pi, r):
-        _, first, count, _, _ = PIECES[ph][pi]
-        slot = 8 if pi == 1 else r % NZ
-        ref = part(ph, r, y, c, first, count)
-        send(ref, ref, y_s.at[ph, slot], y_r.at[ph, slot], side)
-
-    def y_wait(ph, pi, r):
-        _, first, count, _, _ = PIECES[ph][pi]
-        slot = 8 if pi == 1 else r % NZ
-        landed(part(ph, r, 1 - y, c, first, count), y_r.at[ph, slot])
+        landed(part(ph, r, owner_y(piece[0]), c, *span), ring_r.at[ph, way, s, pi], ('ring', ph))
+
+    def y_rows(ph, pi, r, half):
+        _, first, count, last_up, last_down = PIECES[ph][pi]
+        return (first, count) if half is None else (last_up, last_down)[half]
+
+    def y_slot(pi, r, half):
+        return 8 if pi == 1 else (9 if half == 1 else r % NZ)
+
+    def y_send(ph, pi, r, half=None):
+        slot = y_slot(pi, r, half)
+        ref = part(ph, r, y, c, *y_rows(ph, pi, r, half))
+        send(ref, ref, y_s.at[ph, slot], y_r.at[ph, slot], side, ("y", ph))
+
+    def y_wait(ph, pi, r, half=None):
+        landed(part(ph, r, 1 - y, c, *y_rows(ph, pi, r, half)), y_r.at[ph, y_slot(pi, r, half)], ("y", ph))
 
     def twin_send(ph, r, other):
         ref = whole(ph, r, 1 - y if other else y, c)
-        send(ref, ref, sib_s.at[ph, r % NZ, other], sib_r.at[ph, r % NZ, other], twin)
+        send(ref, ref, sib_s.at[ph, r % NZ, other], sib_r.at[ph, r % NZ, other], twin, ("twin", ph))
 
     def twin_wait(ph, r):
         for other in (0, 1):
-            landed(whole(ph, r, 1 - y if other else y, 1 - c), sib_r.at[ph, r % NZ, other])
+            landed(whole(ph, r, 1 - y if other else y, 1 - c), sib_r.at[ph, r % NZ, other], ("twin", ph))
 
     def begin(ph):
         y_send(ph, 1, 0)
@@ -228,36 +238,63 @@
                 ring_send(ph, pi, way, 0)
         y_send(ph, 0, 0)
         twin_send(ph, 0, 0)
+
+    def begin_other(ph):
         y_wait(ph, 1, 0)
         for way in (0, 1):
             ring_send(ph, 2, way, 0)
 
-    def finish_own(ph):
-        y_wait(ph, 0, 0)
-        twin_send(ph, 0, 1)
+    def hop_b(ph, s):
+        for way, r in ((0, -(s + 1)), (1, s + 1)):
+            ring_wait(ph, 0, way, s)
+            if s < 3:
+                ring_send(ph, 0, way, s + 1)
+                y_send(ph, 0, r)
+            else:
+                y_send(ph, 0, 4, way)
+
+    def y_done(ph, r):
+        if r == 4:
+            y_wait(ph, 0, 4, 0)
+            y_wait(ph, 0, 4, 1)
+        else:
+            y_wait(ph, 0, r)
+        twin_send(ph, r, 1)
+
+    def hop_a(ph, s):
+        for way, r in ((0, -(s + 1)), (1, s + 1)):
+            ring_wait(ph, 1, way, s)
+            if s < 3:
+                ring_send(ph, 1, way, s + 1)
+                twin_send(ph, r, 0)
+        if s == 3:
+            twin_send(ph, 4, 0)
+
+    def hop_x(ph, s):
+        for way in (0, 1):
+            ring_wait(ph, 2, way, s)
+            if s < 3:
+                ring_send(ph, 2, way, s + 1)
 
     def hop(ph, s):
-        rels = (-(s + 1), s + 1)
-        for pi in range(3):
-            for way in (0, 1):
-                ring_wait(ph, pi, way, s)
-                if s < 3:
-                    ring_send(ph, pi, way, s + 1)
-                    if pi == 0:
-                        y_send(ph, 0, rels[way])
-                    if pi == 1:
-                        twin_send(ph, rels[way], 0)
-            if s == 3 and pi == 0:
-                y_send(ph, 0, 4)
-            if s == 3 and pi == 1:
-                twin_send(ph, 4, 0)
-        for r in rels if s < 3 else (4,):
-            y_wait(ph, 0, r)
-            twin_send(ph, r, 1)
+        hop_b(ph, s)
+        for r in ((-s, s) if s else (0,)):
+            y_done(ph, r)
+        hop_a(ph, s)
+        hop_x(ph, s)
 
     def project_rel(r):
         twin_wait(0, r)
         project(zrel(r), gq_ref, lt_ref, ltt_ref, p_ref, dp_ref)
+
+    first_head = (9 * zrel(4)) // 2
+
+    def heads(lo, hi):
+        def body(i, carry):
+            attend_head((first_head + 5 + i) % HEADS, p_ref, dp_ref, at_ref, dat_ref)
+            return carry
+
+        lax.fori_loop(lo, hi, body, 0)
 
     for load in loads[:4]:
         load.wait()
@@ -269,8 +306,8 @@
     for load in loads[4:]:
         load.wait()
     normalize(x_ref, t_ref, g_ref, gain_ref, cost_ref, lt_ref, ltt_ref, gt_ref, res_ref)
-
-    finish_own(0)
+    begin_other(0)
+
     hop(0, 0)
     project_rel(0)
     hop(0, 1)
@@ -278,31 +315,39 @@
     project_rel(1)
     hop(0, 2)
     begin(1)
+    begin_other(1)
     project_rel(-2)
     project_rel(2)
-    hop(0, 3)
-    finish_own(1)
+    hop_b(0, 3)
+    hop_a(0, 3)
+    y_done(0, -3)
+    hop_x(0, 3)
+    y_done(0, 3)
     project_rel(-3)
     hop(1, 0)
+    y_done(0, 4)
+    heads(0, 2)
     project_rel(3)
+    hop(1, 1)
+    heads(2, 4)
+    hop(1, 2)
+    heads(4, 7)
     project_rel(4)
-    for s in range(1, 4):
-        hop(1, s)
-        lax.fori_loop(
-            (s - 1) * 4, s * 4, lambda h, carry: (attend_head(h, p_ref, dp_ref, at_ref, dat_ref), carry)[1], 0
-        )
+    hop_b(1, 3)
+    hop_a(1, 3)
+    hop_x(1, 3)
+    y_done(1, -3)
+    y_done(1, 3)
+    heads(7, 10)
+    y_done(1, 4)
+    heads(10, 12)
     for r in range(NZ):
-        twin_wait(1, r)
+        twin_wait(1, r if r <= 4 else r - NZ)
     mine_ref[...] = out_scores(go_ref, at_ref, dat_ref, gt_ref) + res_ref[...]
 
     copies = []
     for k in range(1, NCKPT):
-        copy = pltpu.make_async_remote_copy(
-            src_ref=mine_ref, dst_ref=sums_ref.at[k], send_sem=sum_s.at[k], recv_sem=sum_r.at[k],
-            device_id={"ckpt": (ck + k) % NCKPT}, device_id_type=MESH,
-        )
-        copy.start()
-        copies.append(copy)
+        copies.append(remote(mine_ref, sums_ref.at[k], sum_s.at[k], sum_r.at[k], {"ckpt": (ck + k) % NCKPT}, ("sum", 0)))
     for copy in pending:
         copy.wait_send()
     total = mine_ref[...]
@@ -315,17 +360,19 @@
 
 
 def per_device(states, state_tangent, loss_grad, norm_gain, gain_costate, qkv_weight, qkv_costate, out_weight, out_costate):
-    anywhere = pl.BlockSpec(memory_space=pl.ANY)
+    hbm = pl.BlockSpec(memory_space=pltpu.HBM)
     vmem = pl.BlockSpec(memory_space=pltpu.VMEM)
     out = pl.pallas_call(
         kernel,
         out_shape=jax.ShapeDtypeStruct((1, SEQ), F32),
-        in_specs=[anywhere] * 3 + [vmem] * 2 + [anywhere] * 4,
+        in_specs=[hbm] * 9,
         out_specs=vmem,
         scratch_shapes=[
             pltpu.VMEM((SEQ, D), BF16),
             pltpu.VMEM((SEQ, D), BF16),
             pltpu.VMEM((SEQ, D), BF16),
+            pltpu.VMEM((1, D), BF16),
+            pltpu.VMEM((1, D), BF16),
             pltpu.VMEM((72, D), BF16),
             pltpu.VMEM((72, D), BF16),
             pltpu.VMEM((24, D), BF16),
@@ -342,18 +389,18 @@
             pltpu.VMEM((D, SEQ), BF16),
             pltpu.VMEM((1, SEQ), F32),
             pltpu.VMEM((NCKPT, 1, SEQ), F32),
-            pltpu.SemaphoreType.DMA((7,)),
+            pltpu.SemaphoreType.DMA((9,)),
             pltpu.SemaphoreType.DMA((2, 2, 4, 3)),
             pltpu.SemaphoreType.DMA((2, 2, 4, 3)),
-            pltpu.SemaphoreType.DMA((2, 9)),
-            pltpu.SemaphoreType.DMA((2, 9)),
+            pltpu.SemaphoreType.DMA((2, 10)),
+            pltpu.SemaphoreType.DMA((2, 10)),
             pltpu.SemaphoreType.DMA((2, NZ, 2)),
             pltpu.SemaphoreType.DMA((2, NZ, 2)),
             pltpu.SemaphoreType.DMA((NCKPT,)),
             pltpu.SemaphoreType.DMA((NCKPT,)),
         ],
         compiler_params=pltpu.CompilerParams(
-            collective_id=0, has_side_effects=True, vmem_limit_bytes=48 * 1024 * 1024
+            collective_id=0, has_side_effects=True, vmem_limit_bytes=60 * 1024 * 1024
         ),
         cost_estimate=pl.CostEstimate(flops=9_000_000_000, bytes_accessed=3_000_000, transcendentals=3_200_000),
         name="scores",

time: 90.1 us -> 67.1 us (0.74)
  the two profiles are of different devices: /device:TPU:2 before, /device:TPU:1 now
where the time goes in v2:
time: 67.1 us; the launch traced here: 67 us
  Pallas kernels  65.8 us (98%)
  local copies, waits for them, and re-layouts  1.26 us (2%)
    pallas_call x1, Pallas kernels, per_device(): pl.pallas_call(kernel, out_shape=jax.ShapeDtypeStruct((1, SEQ), F32), in_...  65.8 us

profile of v2, /device:TPU:1, one launch (start us, length us, event | category | flops | bytes accessed | tf_op | source)
XLA Modules:
  0.0 67.0 jit_solution(14933956886819723907)
XLA Ops:
  0.0 65.8 %scores.1 = f32[1,512]{1,0:T(1,128)} custom-call(bf16[1,512,768]{2,1,0:T(8,128)(2,1)} %x_hbm.1, bf16[1,512,768]{2,1,0:T(8,128)(2,1)} %t_hbm.1, bf16[1,512,768]{2,1,0:T(8,128)(2,1)} %g_hbm.1, bf16[1,768]{1,0:T(2,128)(2,1)} %gain_hbm.1, bf16[1,768]{1,0:T(2,128)(2,1)} %cost_hbm.1, bf16[1,72,768]{2,1,0:T(8,128)(2,1)} %wq_hbm.1, bf16[1,72,768]{2,1,0:T(8,128)(2,1)} %cq_hbm.1, ...), custom_call_target="tpu_custom_call" | custom-call | flops 8999999488 | bytes 3000000 | tf_op jit(solution)/shard_map/scores/pallas_call | solution.py:365
  65.8 1.3 %copy.11 = f32[512]{0:T(512)} copy(f32[512]{0:T(512)} %bitcast.1) | data formatting | bytes 4096

commit v3 on v2

--- a/solution.py
+++ b/solution.py
@@ -26,6 +26,18 @@
 PIECES = (
     (("B", 64, 80, (64, 48), (112, 32)), ("A", 0, 64, (0, 32), (32, 32)), ("X", 0, 64, (0, 32), (32, 32))),
     (("B", 16, 32, (16, 16), (32, 16)), ("A", 0, 16, (0, 16), None), ("X", 0, 16, None, (0, 16))),
+)
+
+
+GROUPS = (2, 5, 5)
+ORDER = (
+    "b0", "x0", "b1", "B00d", "B00u", "A00d", "x1", "X00u", "B10d", "N", "B01u", "Y0_0",
+    "X00d", "X01u", "A10d", "B01d", "Y0_-1", "Y0_-2", "A00u", "B10u", "P0", "B11d", "B02u", "X10d",
+    "Y0_1", "A01d", "A10u", "B02d", "Y1_0", "A01u", "X10u", "P1", "B11u", "X01d", "A11d", "Y0_2",
+    "P-2", "Y1_-1", "P-1", "B03u", "X02u", "X11d", "Y0_-3", "B12d", "Y1_1", "Y1_2", "P2", "A11u",
+    "A02d", "A02u", "X02d", "B03d", "X11u", "Y0_3", "B12u", "P-3", "X12d", "H0", "Y1_3", "Y1_-2",
+    "P3", "X03d", "A03u", "A12d", "X03u", "A03d", "B13d", "X12u", "Y0_4", "X13u", "A12u", "T0",
+    "B13u", "H1", "X13d", "Y1_4", "P4", "Y1_-3", "A13u", "A13d", "T1", "H2",
 )
 
 
@@ -82,7 +94,7 @@
     dp_ref[rows, :] = (r2[:, 0:72] + r1[:, 72:144]).reshape(288, SEQ).astype(BF16)
 
 
-def attend_head(h, p_ref, dp_ref, at_ref, dat_ref):
+def head_operands(h, p_ref, dp_ref):
     def rows(base):
         return pl.ds(pl.multiple_of(base + h * HD, HD), HD)
 
@@ -90,29 +102,46 @@
     k, dk = p_ref[rows(D), :], dp_ref[rows(D), :]
     v, dv = p_ref[rows(2 * D), :], dp_ref[rows(2 * D), :]
     kd = jnp.concatenate([k, dk], axis=0).T
+    scale = BF16(1.0 / math.sqrt(HD))
+    q, dq = q * scale, dq * scale
     rhs_s = jnp.concatenate([q, jnp.zeros_like(q)], axis=0)
     rhs_d = jnp.concatenate([dq, q], axis=0)
-    vv = jnp.concatenate([v, dv], axis=0)
-    scale2 = math.log2(math.e) / math.sqrt(HD)
-    for b in range(2):
+    return rows(0), kd, rhs_s, rhs_d, v, jnp.concatenate([v, dv], axis=0)
+
+
+def softmax_block(s, d, upper):
+    n = s.shape[0]
+    diag = jnp.where(upper, s[n - 128 :], NEGATIVE)
+    s = diag if n == 128 else jnp.concatenate([s[: n - 128], diag], axis=0)
+    m = jnp.max(s, axis=0, keepdims=True)
+    e = jnp.exp2((s - m) * math.log2(math.e))
+    a = e * (1.0 / jnp.sum(e, axis=0, keepdims=True))
+    t = jnp.sum(a * d, axis=0, keepdims=True)
+    return a.astype(BF16), (a * (d - t)).astype(BF16)
+
+
+def attend_heads(hs, p_ref, dp_ref, at_ref, dat_ref):
+    row = lax.broadcasted_iota(jnp.int32, (128, 128), 0)
+    col = lax.broadcasted_iota(jnp.int32, (128, 128), 1)
+    upper = row <= col
+    operands = [head_operands(h, p_ref, dp_ref) for h in hs]
+    empty = jnp.zeros((128, 128), BF16)
+    for b in (1, 0):
         cols = slice(256 * b, 256 * b + 256)
-        jm = 256 * (b + 1)
-        s = dot(kd[:jm], rhs_s[:, cols])
-        d = dot(kd[:jm], rhs_d[:, cols])
-        row = lax.broadcasted_iota(jnp.int32, (256, 256), 0)
-        col = lax.broadcasted_iota(jnp.int32, (256, 256), 1)
-        diag = jnp.where(row <= col, s[jm - 256 :], NEGATIVE)
-        s = diag if b == 0 else jnp.concatenate([s[: jm - 256], diag], axis=0)
-        m = jnp.max(s, axis=0, keepdims=True)
-        e = jnp.exp2((s - m) * scale2)
-        r = 1.0 / jnp.sum(e, axis=0, keepdims=True)
-        t = jnp.sum(e * d, axis=0, keepdims=True) * r
-        a = (e * r).astype(BF16)
-        da = ((e * (r * (1.0 / math.sqrt(HD)))) * (d - t)).astype(BF16)
-        o1 = dot(vv[:, :jm], a)
-        o2 = dot(v[:, :jm], da)
-        at_ref[rows(0), cols] = o1[:HD].astype(BF16)
-        dat_ref[rows(0), cols] = (o1[HD:] + o2).astype(BF16)
+        n = 256 * (b + 1)
+        logits = [(dot(kd[:n], rs[:, cols]), dot(kd[:n], rd[:, cols])) for _, kd, rs, rd, _, _ in operands]
+        weights = []
+        for s, d in logits:
+            left = softmax_block(s[: n - 128, :128], d[: n - 128, :128], upper)
+            right = softmax_block(s[:, 128:], d[:, 128:], upper)
+            weights.append(
+                [jnp.concatenate([jnp.concatenate([l, empty], axis=0), r], axis=1) for l, r in zip(left, right)]
+            )
+        for (rows, _, _, _, v, vv), (a, da) in zip(operands, weights):
+            o1 = dot(vv[:, :n], a)
+            o2 = dot(v[:, :n], da)
+            at_ref[rows, cols] = o1[:HD].astype(BF16)
+            dat_ref[rows, cols] = (o1[HD:] + o2).astype(BF16)
 
 
 def out_scores(go_ref, at_ref, dat_ref, gt_ref):
@@ -198,7 +227,7 @@
             return
         r = -s if way == 0 else s
         ref = part(ph, r, owner_y(piece[0]), c, *span)
-        send(ref, ref, ring_s.at[ph, way, s, pi], ring_r.at[ph, way, s, pi], up if way == 0 else down, ('ring', ph))
+        send(ref, ref, ring_s.at[ph, way, s, pi], ring_r.at[ph, way, s, pi], up if way == 0 else down, ("ring", ph, pi, way, s))
 
     def ring_wait(ph, pi, way, s):
         piece = PIECES[ph][pi]
@@ -206,7 +235,7 @@
         if span is None:
             return
         r = -(s + 1) if way == 0 else s + 1
-        landed(part(ph, r, owner_y(piece[0]), c, *span), ring_r.at[ph, way, s, pi], ('ring', ph))
+        landed(part(ph, r, owner_y(piece[0]), c, *span), ring_r.at[ph, way, s, pi], ("ring", ph, pi, way, s))
 
     def y_rows(ph, pi, r, half):
         _, first, count, last_up, last_down = PIECES[ph][pi]
@@ -218,18 +247,18 @@
     def y_send(ph, pi, r, half=None):
         slot = y_slot(pi, r, half)
         ref = part(ph, r, y, c, *y_rows(ph, pi, r, half))
-        send(ref, ref, y_s.at[ph, slot], y_r.at[ph, slot], side, ("y", ph))
+        send(ref, ref, y_s.at[ph, slot], y_r.at[ph, slot], side, ("y", ph, slot))
 
     def y_wait(ph, pi, r, half=None):
-        landed(part(ph, r, 1 - y, c, *y_rows(ph, pi, r, half)), y_r.at[ph, y_slot(pi, r, half)], ("y", ph))
+        landed(part(ph, r, 1 - y, c, *y_rows(ph, pi, r, half)), y_r.at[ph, y_slot(pi, r, half)], ("y", ph, y_slot(pi, r, half)))
 
     def twin_send(ph, r, other):
         ref = whole(ph, r, 1 - y if other else y, c)
-        send(ref, ref, sib_s.at[ph, r % NZ, other], sib_r.at[ph, r % NZ, other], twin, ("twin", ph))
+        send(ref, ref, sib_s.at[ph, r % NZ, other], sib_r.at[ph, r % NZ, other], twin, ("twin", ph, r % NZ, other))
 
     def twin_wait(ph, r):
         for other in (0, 1):
-            landed(whole(ph, r, 1 - y if other else y, 1 - c), sib_r.at[ph, r % NZ, other], ("twin", ph))
+            landed(whole(ph, r, 1 - y if other else y, 1 - c), sib_r.at[ph, r % NZ, other], ("twin", ph, r % NZ, other))
 
     def begin(ph):
         y_send(ph, 1, 0)
@@ -244,14 +273,17 @@
         for way in (0, 1):
             ring_send(ph, 2, way, 0)
 
-    def hop_b(ph, s):
-        for way, r in ((0, -(s + 1)), (1, s + 1)):
-            ring_wait(ph, 0, way, s)
-            if s < 3:
-                ring_send(ph, 0, way, s + 1)
+    def ring_step(ph, pi, s, way):
+        ring_wait(ph, pi, way, s)
+        r = -(s + 1) if way == 0 else s + 1
+        if s < 3:
+            ring_send(ph, pi, way, s + 1)
+            if pi == 0:
                 y_send(ph, 0, r)
-            else:
-                y_send(ph, 0, 4, way)
+            if pi == 1:
+                twin_send(ph, r, 0)
+        elif pi == 0:
+            y_send(ph, 0, 4, way)
 
     def y_done(ph, r):
         if r == 4:
@@ -261,93 +293,54 @@
             y_wait(ph, 0, r)
         twin_send(ph, r, 1)
 
-    def hop_a(ph, s):
-        for way, r in ((0, -(s + 1)), (1, s + 1)):
-            ring_wait(ph, 1, way, s)
-            if s < 3:
-                ring_send(ph, 1, way, s + 1)
-                twin_send(ph, r, 0)
-        if s == 3:
-            twin_send(ph, 4, 0)
-
-    def hop_x(ph, s):
-        for way in (0, 1):
-            ring_wait(ph, 2, way, s)
-            if s < 3:
-                ring_send(ph, 2, way, s + 1)
-
-    def hop(ph, s):
-        hop_b(ph, s)
-        for r in ((-s, s) if s else (0,)):
-            y_done(ph, r)
-        hop_a(ph, s)
-        hop_x(ph, s)
-
     def project_rel(r):
         twin_wait(0, r)
         project(zrel(r), gq_ref, lt_ref, ltt_ref, p_ref, dp_ref)
 
     first_head = (9 * zrel(4)) // 2
 
-    def heads(lo, hi):
-        def body(i, carry):
-            attend_head((first_head + 5 + i) % HEADS, p_ref, dp_ref, at_ref, dat_ref)
-            return carry
-
-        lax.fori_loop(lo, hi, body, 0)
+    def head_group(k):
+        first = first_head + 5 + sum(GROUPS[:k])
+        attend_heads([(first + j) % HEADS for j in range(GROUPS[k])], p_ref, dp_ref, at_ref, dat_ref)
+
+    def load_rest():
+        for load in loads[4:]:
+            load.wait()
+        normalize(x_ref, t_ref, g_ref, gain_ref, cost_ref, lt_ref, ltt_ref, gt_ref, res_ref)
+
+    def run(op):
+        kind = op[0]
+        if kind in "BAX":
+            ring_step(int(op[1]), "BAX".index(kind), int(op[2]), "ud".index(op[3]))
+        elif kind == "b":
+            begin(int(op[1]))
+        elif kind == "x":
+            begin_other(int(op[1]))
+        elif kind == "Y":
+            y_done(int(op[1]), int(op[3:]))
+        elif kind == "T":
+            twin_send(int(op[1]), 4, 0)
+        elif kind == "P":
+            project_rel(int(op[1:]))
+        elif kind == "H":
+            head_group(int(op[1:]))
+        elif kind == "N":
+            load_rest()
 
     for load in loads[:4]:
         load.wait()
     gq_ref[me] = jnp.concatenate([wq_ref[...].astype(F32), cq_ref[...].astype(F32)], axis=0).astype(BF16)
     go_ref[me] = jnp.concatenate([wo_ref[...].astype(F32), co_ref[...].astype(F32)], axis=0).astype(BF16)
     pl.semaphore_wait(barrier, 4 + NCKPT - 1)
-    begin(0)
-
-    for load in loads[4:]:
-        load.wait()
-    normalize(x_ref, t_ref, g_ref, gain_ref, cost_ref, lt_ref, ltt_ref, gt_ref, res_ref)
-    begin_other(0)
-
-    hop(0, 0)
-    project_rel(0)
-    hop(0, 1)
-    project_rel(-1)
-    project_rel(1)
-    hop(0, 2)
-    begin(1)
-    begin_other(1)
-    project_rel(-2)
-    project_rel(2)
-    hop_b(0, 3)
-    hop_a(0, 3)
-    y_done(0, -3)
-    hop_x(0, 3)
-    y_done(0, 3)
-    project_rel(-3)
-    hop(1, 0)
-    y_done(0, 4)
-    heads(0, 2)
-    project_rel(3)
-    hop(1, 1)
-    heads(2, 4)
-    hop(1, 2)
-    heads(4, 7)
-    project_rel(4)
-    hop_b(1, 3)
-    hop_a(1, 3)
-    hop_x(1, 3)
-    y_done(1, -3)
-    y_done(1, 3)
-    heads(7, 10)
-    y_done(1, 4)
-    heads(10, 12)
+    for op in ORDER:
+        run(op)
     for r in range(NZ):
         twin_wait(1, r if r <= 4 else r - NZ)
     mine_ref[...] = out_scores(go_ref, at_ref, dat_ref, gt_ref) + res_ref[...]
 
     copies = []
     for k in range(1, NCKPT):
-        copies.append(remote(mine_ref, sums_ref.at[k], sum_s.at[k], sum_r.at[k], {"ckpt": (ck + k) % NCKPT}, ("sum", 0)))
+        copies.append(remote(mine_ref, sums_ref.at[k], sum_s.at[k], sum_r.at[k], {"ckpt": (ck + k) % NCKPT}, ("sum", 0, 0)))
     for copy in pending:
         copy.wait_send()
     total = mine_ref[...]

time: 67.1 us -> 59 us (0.88)
  Pallas kernels: 65.8 us -> 57.6 us
    pallas_call x1, Pallas kernels: 65.8 us -> 57.6 us  [per_device(): pl.pallas_call(kernel, out_shape=jax.ShapeDtypeStruct((1, SEQ), F32), in_...]
where the time goes in v3:
time: 59 us; the launch traced here: 58.9 us
  Pallas kernels  57.6 us (98%)
  local copies, waits for them, and re-layouts  1.26 us (2%)
    pallas_call x1, Pallas kernels, per_device(): pl.pallas_call(kernel, out_shape=jax.ShapeDtypeStruct((1, SEQ), F32), in_...  57.6 us
    unnamed x1, local copies, waits for them, and re-layouts  1.26 us

profile of v3, /device:TPU:1, one launch (start us, length us, event | category | flops | bytes accessed | tf_op | source)
XLA Modules:
  0.0 58.9 jit_solution(949784191008244518)
XLA Ops:
  0.0 57.6 %scores.1 = f32[1,512]{1,0:T(1,128)} custom-call(bf16[1,512,768]{2,1,0:T(8,128)(2,1)} %x_hbm.1, bf16[1,512,768]{2,1,0:T(8,128)(2,1)} %t_hbm.1, bf16[1,512,768]{2,1,0:T(8,128)(2,1)} %g_hbm.1, bf16[1,768]{1,0:T(2,128)(2,1)} %gain_hbm.1, bf16[1,768]{1,0:T(2,128)(2,1)} %cost_hbm.1, bf16[1,72,768]{2,1,0:T(8,128)(2,1)} %wq_hbm.1, bf16[1,72,768]{2,1,0:T(8,128)(2,1)} %cq_hbm.1, ...), custom_call_target="tpu_custom_call" | custom-call | flops 8999999488 | bytes 3000000 | tf_op jit(solution)/shard_map/scores/pallas_call | solution.py:358
  57.6 1.3 %copy.11 = f32[512]{0:T(512)} copy(f32[512]{0:T(512)} %bitcast.1) | data formatting | bytes 4096

commit v4 on v3

--- a/solution.py
+++ b/solution.py
@@ -29,15 +29,15 @@
 )
 
 
-GROUPS = (2, 5, 5)
+GROUPS = (2, 3, 2, 5)
 ORDER = (
-    "b0", "x0", "b1", "B00d", "B00u", "A00d", "x1", "X00u", "B10d", "N", "B01u", "Y0_0",
-    "X00d", "X01u", "A10d", "B01d", "Y0_-1", "Y0_-2", "A00u", "B10u", "P0", "B11d", "B02u", "X10d",
-    "Y0_1", "A01d", "A10u", "B02d", "Y1_0", "A01u", "X10u", "P1", "B11u", "X01d", "A11d", "Y0_2",
-    "P-2", "Y1_-1", "P-1", "B03u", "X02u", "X11d", "Y0_-3", "B12d", "Y1_1", "Y1_2", "P2", "A11u",
-    "A02d", "A02u", "X02d", "B03d", "X11u", "Y0_3", "B12u", "P-3", "X12d", "H0", "Y1_3", "Y1_-2",
-    "P3", "X03d", "A03u", "A12d", "X03u", "A03d", "B13d", "X12u", "Y0_4", "X13u", "A12u", "T0",
-    "B13u", "H1", "X13d", "Y1_4", "P4", "Y1_-3", "A13u", "A13d", "T1", "H2",
+    "b1", "b0", "N", "x1", "Y1_0", "B10d", "A10d", "x0", "B00d", "B00u", "Y0_0", "A00u",
+    "A00d", "X00u", "B11d", "B01u", "X00d", "P0", "B01d", "Y0_-1", "Y0_1", "P-1", "B10u", "A11d",
+    "X10d", "A01d", "A01u", "X01u", "Y0_-2", "X01d", "X10u", "Y1_1", "B02u", "Y0_2", "Y1_-1", "B02d",
+    "A10u", "P2", "B11u", "B12d", "P1", "A12d", "A02u", "X02u", "Y0_-3", "P-2", "X11u", "X11d",
+    "A02d", "Y1_2", "P-3", "B03u", "X02d", "Y0_3", "H0", "A11u", "B03d", "B12u", "P3", "X12d",
+    "B13d", "H2", "Y1_3", "A13d", "A03d", "X03u", "Y1_-2", "X12u", "A03u", "X13u", "A12u", "X03d",
+    "T0", "Y0_4", "B13u", "H1", "P4", "Y1_-3", "A13u", "T1", "X13d", "Y1_4", "H3",
 )
 
 
@@ -161,7 +161,7 @@
     x_ref, t_ref, g_ref, gain_ref, cost_ref, wq_ref, cq_ref, wo_ref, co_ref,
     gq_ref, go_ref, lt_ref, ltt_ref, gt_ref, res_ref, p_ref, dp_ref, at_ref, dat_ref,
     mine_ref, sums_ref,
-    in_sem, ring_s, ring_r, y_s, y_r, sib_s, sib_r, sum_s, sum_r,
+    in_sem, sent, ring_r, y_r, twin_r, sum_r,
 ):
     ck = lax.axis_index("ckpt")
     me = lax.axis_index("fsdp")
@@ -180,18 +180,12 @@
     side = dev(z, 1 - y, c)
     twin = dev(z, y, 1 - c)
 
-    loads = [
-        pltpu.make_async_copy(src, dst, in_sem.at[i])
-        for i, (src, dst) in enumerate(
-            (
-                (wq_hbm.at[0], wq_ref), (cq_hbm.at[0], cq_ref), (wo_hbm.at[0], wo_ref), (co_hbm.at[0], co_ref),
-                (x_hbm.at[0], x_ref), (t_hbm.at[0], t_ref), (gain_hbm, gain_ref), (cost_hbm, cost_ref),
-                (g_hbm.at[0], g_ref),
-            )
-        )
-    ]
-    for load in loads:
-        load.start()
+    for i, src, dst in (
+        (0, wq_hbm.at[0], wq_ref), (0, cq_hbm.at[0], cq_ref), (0, wo_hbm.at[0], wo_ref), (0, co_hbm.at[0], co_ref),
+        (1, x_hbm.at[0], x_ref), (1, t_hbm.at[0], t_ref), (1, g_hbm.at[0], g_ref),
+        (2, gain_hbm, gain_ref), (3, cost_hbm, cost_ref),
+    ):
+        pltpu.make_async_copy(src, dst, in_sem.at[i]).start()
 
     barrier = pltpu.get_barrier_semaphore()
     for peer in (up, down, side, twin):
@@ -200,10 +194,9 @@
         pl.semaphore_signal(barrier, inc=1, device_id={"ckpt": (ck + k) % NCKPT}, device_id_type=MESH)
 
     bufs = (gq_ref, go_ref)
-    pending = []
-
-    def send(src, dst, ssem, rsem, peer, tag):
-        pending.append(remote(src, dst, ssem, rsem, {"fsdp": peer}, tag))
+
+    def send(ref, slot, rsem, peer, tag):
+        remote(ref, ref, sent.at[slot], rsem, {"fsdp": peer}, tag)
 
     def part(ph, r, yy, cc, first, count):
         return bufs[ph].at[dev(zrel(r), yy, cc), pl.ds(first, count), :]
@@ -227,7 +220,7 @@
             return
         r = -s if way == 0 else s
         ref = part(ph, r, owner_y(piece[0]), c, *span)
-        send(ref, ref, ring_s.at[ph, way, s, pi], ring_r.at[ph, way, s, pi], up if way == 0 else down, ("ring", ph, pi, way, s))
+        send(ref, 0, ring_r.at[ph, way, s, pi], up if way == 0 else down, ("ring", ph, pi, way, s))
 
     def ring_wait(ph, pi, way, s):
         piece = PIECES[ph][pi]
@@ -241,24 +234,24 @@
         _, first, count, last_up, last_down = PIECES[ph][pi]
         return (first, count) if half is None else (last_up, last_down)[half]
 
-    def y_slot(pi, r, half):
-        return 8 if pi == 1 else (9 if half == 1 else r % NZ)
+    def y_slot(pi, r):
+        return 8 if pi == 1 else r % NZ
 
     def y_send(ph, pi, r, half=None):
-        slot = y_slot(pi, r, half)
+        slot = y_slot(pi, r)
         ref = part(ph, r, y, c, *y_rows(ph, pi, r, half))
-        send(ref, ref, y_s.at[ph, slot], y_r.at[ph, slot], side, ("y", ph, slot))
-
-    def y_wait(ph, pi, r, half=None):
-        landed(part(ph, r, 1 - y, c, *y_rows(ph, pi, r, half)), y_r.at[ph, y_slot(pi, r, half)], ("y", ph, y_slot(pi, r, half)))
+        send(ref, 0, y_r.at[ph, slot], side, ("y", ph, slot))
+
+    def y_wait(ph, pi, r):
+        slot = y_slot(pi, r)
+        landed(part(ph, r, 1 - y, c, *y_rows(ph, pi, r, None)), y_r.at[ph, slot], ("y", ph, slot))
 
     def twin_send(ph, r, other):
         ref = whole(ph, r, 1 - y if other else y, c)
-        send(ref, ref, sib_s.at[ph, r % NZ, other], sib_r.at[ph, r % NZ, other], twin, ("twin", ph, r % NZ, other))
-
-    def twin_wait(ph, r):
-        for other in (0, 1):
-            landed(whole(ph, r, 1 - y if other else y, 1 - c), sib_r.at[ph, r % NZ, other], ("twin", ph, r % NZ, other))
+        send(ref, 1 + ph, twin_r.at[r % NZ if ph == 0 else NZ], twin, ("twin", ph, r % NZ, other))
+
+    def twin_wait(r):
+        landed(gq_ref.at[pl.ds(0, 2)], twin_r.at[r % NZ], ("twin", 0, r % NZ))
 
     def begin(ph):
         y_send(ph, 1, 0)
@@ -286,15 +279,11 @@
             y_send(ph, 0, 4, way)
 
     def y_done(ph, r):
-        if r == 4:
-            y_wait(ph, 0, 4, 0)
-            y_wait(ph, 0, 4, 1)
-        else:
-            y_wait(ph, 0, r)
+        y_wait(ph, 0, r)
         twin_send(ph, r, 1)
 
     def project_rel(r):
-        twin_wait(0, r)
+        twin_wait(r)
         project(zrel(r), gq_ref, lt_ref, ltt_ref, p_ref, dp_ref)
 
     first_head = (9 * zrel(4)) // 2
@@ -304,8 +293,9 @@
         attend_heads([(first + j) % HEADS for j in range(GROUPS[k])], p_ref, dp_ref, at_ref, dat_ref)
 
     def load_rest():
-        for load in loads[4:]:
-            load.wait()
+        landed(go_ref, in_sem.at[1], ("in", 0))
+        landed(gain_ref, in_sem.at[2], ("in", 0))
+        landed(cost_ref, in_sem.at[3], ("in", 0))
         normalize(x_ref, t_ref, g_ref, gain_ref, cost_ref, lt_ref, ltt_ref, gt_ref, res_ref)
 
     def run(op):
@@ -327,29 +317,26 @@
         elif kind == "N":
             load_rest()
 
-    for load in loads[:4]:
-        load.wait()
+    landed(x_ref.at[pl.ds(0, 192)], in_sem.at[0], ("in", 0))
     gq_ref[me] = jnp.concatenate([wq_ref[...].astype(F32), cq_ref[...].astype(F32)], axis=0).astype(BF16)
     go_ref[me] = jnp.concatenate([wo_ref[...].astype(F32), co_ref[...].astype(F32)], axis=0).astype(BF16)
     pl.semaphore_wait(barrier, 4 + NCKPT - 1)
     for op in ORDER:
         run(op)
-    for r in range(NZ):
-        twin_wait(1, r if r <= 4 else r - NZ)
+    landed(go_ref.at[pl.ds(0, 16)], twin_r.at[NZ], ("twin", 1))
     mine_ref[...] = out_scores(go_ref, at_ref, dat_ref, gt_ref) + res_ref[...]
 
-    copies = []
     for k in range(1, NCKPT):
-        copies.append(remote(mine_ref, sums_ref.at[k], sum_s.at[k], sum_r.at[k], {"ckpt": (ck + k) % NCKPT}, ("sum", 0, 0)))
-    for copy in pending:
-        copy.wait_send()
+        remote(mine_ref, sums_ref.at[k], sent.at[3], sum_r.at[k], {"ckpt": (ck + k) % NCKPT}, ("sum", 0, k))
+    landed(gq_ref.at[pl.ds(0, 20)], sent.at[0], ("sent", 0))
+    landed(gq_ref.at[pl.ds(0, 16)], sent.at[1], ("sent", 1))
+    landed(go_ref.at[pl.ds(0, 16)], sent.at[2], ("sent", 2))
     total = mine_ref[...]
-    for k, copy in enumerate(copies):
-        copy.wait_recv()
-        total = total + sums_ref[k + 1]
+    for k in range(1, NCKPT):
+        landed(sums_ref.at[k], sum_r.at[k], ("sum", 0, k))
+        total = total + sums_ref[k]
     out_ref[...] = total
-    for copy in copies:
-        copy.wait_send()
+    landed(sums_ref.at[pl.ds(1, NCKPT - 1)], sent.at[3], ("sent", 3))
 
 
 def per_device(states, state_tangent, loss_grad, norm_gain, gain_costate, qkv_weight, qkv_costate, out_weight, out_costate):
@@ -382,14 +369,11 @@
             pltpu.VMEM((D, SEQ), BF16),
             pltpu.VMEM((1, SEQ), F32),
             pltpu.VMEM((NCKPT, 1, SEQ), F32),
-            pltpu.SemaphoreType.DMA((9,)),
+            pltpu.SemaphoreType.DMA((4,)),
+            pltpu.SemaphoreType.DMA((4,)),
             pltpu.SemaphoreType.DMA((2, 2, 4, 3)),
-            pltpu.SemaphoreType.DMA((2, 2, 4, 3)),
-            pltpu.SemaphoreType.DMA((2, 10)),
-            pltpu.SemaphoreType.DMA((2, 10)),
-            pltpu.SemaphoreType.DMA((2, NZ, 2)),
-            pltpu.SemaphoreType.DMA((2, NZ, 2)),
-            pltpu.SemaphoreType.DMA((NCKPT,)),
+            pltpu.SemaphoreType.DMA((2, 9)),
+            pltpu.SemaphoreType.DMA((NZ + 1,)),
             pltpu.SemaphoreType.DMA((NCKPT,)),
         ],
         compiler_params=pltpu.CompilerParams(

time: 59 us -> 57.3 us (0.971)
  Pallas kernels: 57.6 us -> 55.9 us
    pallas_call x1, Pallas kernels: 57.6 us -> 55.9 us  [per_device(): pl.pallas_call(kernel, out_shape=jax.ShapeDtypeStruct((1, SEQ), F32), in_...]
where the time goes in v4:
time: 57.3 us; the launch traced here: 57.2 us
  Pallas kernels  55.9 us (98%)
  local copies, waits for them, and re-layouts  1.26 us (2%)
    pallas_call x1, Pallas kernels, per_device(): pl.pallas_call(kernel, out_shape=jax.ShapeDtypeStruct((1, SEQ), F32), in_...  55.9 us
    unnamed x1, local copies, waits for them, and re-layouts  1.26 us

profile of v4, /device:TPU:1, one launch (start us, length us, event | category | flops | bytes accessed | tf_op | source)
XLA Modules:
  0.0 57.2 jit_solution(9172774808124824029)
XLA Ops:
  0.0 55.9 %scores.1 = f32[1,512]{1,0:T(1,128)} custom-call(bf16[1,512,768]{2,1,0:T(8,128)(2,1)} %x_hbm.1, bf16[1,512,768]{2,1,0:T(8,128)(2,1)} %t_hbm.1, bf16[1,512,768]{2,1,0:T(8,128)(2,1)} %g_hbm.1, bf16[1,768]{1,0:T(2,128)(2,1)} %gain_hbm.1, bf16[1,768]{1,0:T(2,128)(2,1)} %cost_hbm.1, bf16[1,72,768]{2,1,0:T(8,128)(2,1)} %wq_hbm.1, bf16[1,72,768]{2,1,0:T(8,128)(2,1)} %cq_hbm.1, ...), custom_call_target="tpu_custom_call" | custom-call | flops 8999999488 | bytes 3000000 | tf_op jit(solution)/shard_map/scores/pallas_call | solution.py:345
  55.9 1.3 %copy.11 = f32[512]{0:T(512)} copy(f32[512]{0:T(512)} %bitcast.1) | data formatting | bytes 4096

commit v5 on v4

--- a/solution.py
+++ b/solution.py
@@ -29,15 +29,17 @@
 )
 
 
+OUT_GROUPS = ((0, -1, 1), (-2, 2), (3, -3), (4,))
 GROUPS = (2, 3, 2, 5)
 ORDER = (
-    "b1", "b0", "N", "x1", "Y1_0", "B10d", "A10d", "x0", "B00d", "B00u", "Y0_0", "A00u",
-    "A00d", "X00u", "B11d", "B01u", "X00d", "P0", "B01d", "Y0_-1", "Y0_1", "P-1", "B10u", "A11d",
-    "X10d", "A01d", "A01u", "X01u", "Y0_-2", "X01d", "X10u", "Y1_1", "B02u", "Y0_2", "Y1_-1", "B02d",
-    "A10u", "P2", "B11u", "B12d", "P1", "A12d", "A02u", "X02u", "Y0_-3", "P-2", "X11u", "X11d",
-    "A02d", "Y1_2", "P-3", "B03u", "X02d", "Y0_3", "H0", "A11u", "B03d", "B12u", "P3", "X12d",
-    "B13d", "H2", "Y1_3", "A13d", "A03d", "X03u", "Y1_-2", "X12u", "A03u", "X13u", "A12u", "X03d",
-    "T0", "Y0_4", "B13u", "H1", "P4", "Y1_-3", "A13u", "T1", "X13d", "Y1_4", "H3",
+    "b1", "b0", "x1", "Y1_0", "x0", "B00u", "A00u", "B00d", "B10d", "A10d", "A00d", "Y0_0",
+    "X00u", "Y0_-1", "X00d", "Y0_1", "B01u", "B01d", "N", "X10d", "B10u", "P0", "A01u", "X01u",
+    "P1", "Y0_-2", "A10u", "B02u", "X01d", "Y0_2", "Y1_1", "X10u", "B02d", "A01d", "Y1_-1", "B11u",
+    "P-1", "A02u", "B11d", "P2", "A11d", "X11d", "U0", "X02u", "Y0_-3", "X02d", "P-2", "A11u",
+    "B03d", "P-3", "A02d", "B03u", "Y0_3", "H0", "B12d", "X11u", "A12d", "B12u", "Y1_-2", "Y1_2",
+    "X12d", "P3", "H2", "A03u", "X03u", "U1", "B13d", "A12u", "A13d", "X03d", "Y0_4", "A03d",
+    "T0", "X13d", "B13u", "H1", "X12u", "X13u", "Y1_3", "P4", "Y1_4", "Y1_-3", "A13u", "T1",
+    "H3", "U3", "U2",
 )
 
 
@@ -74,7 +76,7 @@
         lifted_t = (cost * normed + gain * normed_t).astype(BF16)
         lt_ref[:, rows] = lifted.T
         ltt_ref[:, rows] = lifted_t.T
-        gt_ref[:, rows] = g.T
+        gt_ref[:, rows] = g_ref[rows, :].T
         p = g * t
         q = p[:, 0:128]
         for k in range(1, D // 128):
@@ -144,14 +146,21 @@
             dat_ref[rows, cols] = (o1[HD:] + o2).astype(BF16)
 
 
-def out_scores(go_ref, at_ref, dat_ref, gt_ref):
+def grad_times_out(zcs, first, go_ref, gt_ref, u_ref, uc_ref):
+    blocks = [go_ref[pl.ds(zc * 4, 4)].astype(F32) for zc in zcs]
+    grad = jnp.concatenate([gt_ref[pl.ds(pl.multiple_of(zc * 96, 96), 96), :] for zc in zcs], axis=0)
+    for lo, ref in ((0, u_ref), (24, uc_ref)):
+        w = jnp.concatenate([b[:, lo : lo + 24].reshape(96, D) for b in blocks], axis=0).astype(BF16)
+        term = dot(w.T, grad)
+        ref[...] = term if first else ref[...] + term
+
+
+def out_scores(at_ref, dat_ref, u_ref, uc_ref):
     total = jnp.zeros((1, SEQ), F32)
-    for b in range(2):
-        devs = slice(16 * b, 16 * b + 16)
-        r1 = dot(go_ref[devs, 0:32, :].reshape(512, D), dat_ref[...]).reshape(16, 32, SEQ)
-        r2 = dot(go_ref[devs, 16:48, :].reshape(512, D), at_ref[...]).reshape(16, 32, SEQ)
-        po = (r1[:, 0:24] + r2[:, 8:32]).reshape(384, SEQ)
-        total = total + jnp.sum(po * gt_ref[384 * b : 384 * b + 384, :], axis=0, keepdims=True)
+    for i in range(0, D, 128):
+        rows = slice(i, i + 128)
+        term = dat_ref[rows, :].astype(F32) * u_ref[rows, :] + at_ref[rows, :].astype(F32) * uc_ref[rows, :]
+        total = total + jnp.sum(term, axis=0, keepdims=True)
     return total
 
 
@@ -159,7 +168,7 @@
     x_hbm, t_hbm, g_hbm, gain_hbm, cost_hbm, wq_hbm, cq_hbm, wo_hbm, co_hbm,
     out_ref,
     x_ref, t_ref, g_ref, gain_ref, cost_ref, wq_ref, cq_ref, wo_ref, co_ref,
-    gq_ref, go_ref, lt_ref, ltt_ref, gt_ref, res_ref, p_ref, dp_ref, at_ref, dat_ref,
+    gq_ref, go_ref, lt_ref, ltt_ref, gt_ref, res_ref, p_ref, dp_ref, at_ref, dat_ref, u_ref, uc_ref,
     mine_ref, sums_ref,
     in_sem, sent, ring_r, y_r, twin_r, sum_r,
 ):
@@ -180,18 +189,20 @@
     side = dev(z, 1 - y, c)
     twin = dev(z, y, 1 - c)
 
+    barrier = pltpu.get_barrier_semaphore()
+    for peer in (up, down, side, twin):
+        pl.semaphore_signal(barrier, inc=1, device_id={"fsdp": peer}, device_id_type=MESH)
     for i, src, dst in (
-        (0, wq_hbm.at[0], wq_ref), (0, cq_hbm.at[0], cq_ref), (0, wo_hbm.at[0], wo_ref), (0, co_hbm.at[0], co_ref),
+        (0, wq_hbm.at[0], wq_ref), (0, cq_hbm.at[0], cq_ref), (4, wo_hbm.at[0], wo_ref), (4, co_hbm.at[0], co_ref),
+    ):
+        pltpu.make_async_copy(src, dst, in_sem.at[i]).start()
+    for k in range(1, NCKPT):
+        pl.semaphore_signal(barrier, inc=1, device_id={"ckpt": (ck + k) % NCKPT}, device_id_type=MESH)
+    for i, src, dst in (
         (1, x_hbm.at[0], x_ref), (1, t_hbm.at[0], t_ref), (1, g_hbm.at[0], g_ref),
         (2, gain_hbm, gain_ref), (3, cost_hbm, cost_ref),
     ):
         pltpu.make_async_copy(src, dst, in_sem.at[i]).start()
-
-    barrier = pltpu.get_barrier_semaphore()
-    for peer in (up, down, side, twin):
-        pl.semaphore_signal(barrier, inc=1, device_id={"fsdp": peer}, device_id_type=MESH)
-    for k in range(1, NCKPT):
-        pl.semaphore_signal(barrier, inc=1, device_id={"ckpt": (ck + k) % NCKPT}, device_id_type=MESH)
 
     bufs = (gq_ref, go_ref)
 
@@ -248,12 +259,15 @@
 
     def twin_send(ph, r, other):
         ref = whole(ph, r, 1 - y if other else y, c)
-        send(ref, 1 + ph, twin_r.at[r % NZ if ph == 0 else NZ], twin, ("twin", ph, r % NZ, other))
-
-    def twin_wait(r):
-        landed(gq_ref.at[pl.ds(0, 2)], twin_r.at[r % NZ], ("twin", 0, r % NZ))
+        send(ref, 1 + ph, twin_r.at[ph, r % NZ], twin, ("twin", ph, r % NZ, other))
+
+    def twin_wait(ph, r):
+        landed(bufs[ph].at[pl.ds(0, 2)], twin_r.at[ph, r % NZ], ("twin", ph, r % NZ))
 
     def begin(ph):
+        if ph == 1:
+            landed(go_ref.at[0], in_sem.at[4], ("in", 0))
+            go_ref[me] = jnp.concatenate([wo_ref[...].astype(F32), co_ref[...].astype(F32)], axis=0).astype(BF16)
         y_send(ph, 1, 0)
         for pi in (0, 1):
             for way in (0, 1):
@@ -283,8 +297,13 @@
         twin_send(ph, r, 1)
 
     def project_rel(r):
-        twin_wait(r)
+        twin_wait(0, r)
         project(zrel(r), gq_ref, lt_ref, ltt_ref, p_ref, dp_ref)
+
+    def out_group(k):
+        for r in OUT_GROUPS[k]:
+            twin_wait(1, r)
+        grad_times_out([zrel(r) for r in OUT_GROUPS[k]], k == 0, go_ref, gt_ref, u_ref, uc_ref)
 
     first_head = (9 * zrel(4)) // 2
 
@@ -314,17 +333,17 @@
             project_rel(int(op[1:]))
         elif kind == "H":
             head_group(int(op[1:]))
+        elif kind == "U":
+            out_group(int(op[1]))
         elif kind == "N":
             load_rest()
 
-    landed(x_ref.at[pl.ds(0, 192)], in_sem.at[0], ("in", 0))
+    landed(gq_ref.at[0], in_sem.at[0], ("in", 0))
     gq_ref[me] = jnp.concatenate([wq_ref[...].astype(F32), cq_ref[...].astype(F32)], axis=0).astype(BF16)
-    go_ref[me] = jnp.concatenate([wo_ref[...].astype(F32), co_ref[...].astype(F32)], axis=0).astype(BF16)
     pl.semaphore_wait(barrier, 4 + NCKPT - 1)
     for op in ORDER:
         run(op)
-    landed(go_ref.at[pl.ds(0, 16)], twin_r.at[NZ], ("twin", 1))
-    mine_ref[...] = out_scores(go_ref, at_ref, dat_ref, gt_ref) + res_ref[...]
+    mine_ref[...] = out_scores(at_ref, dat_ref, u_ref, uc_ref) + res_ref[...]
 
     for k in range(1, NCKPT):
         remote(mine_ref, sums_ref.at[k], sent.at[3], sum_r.at[k], {"ckpt": (ck + k) % NCKPT}, ("sum", 0, k))
@@ -361,19 +380,21 @@
             pltpu.VMEM((NDEV, RO, D), BF16),
             pltpu.VMEM((D, SEQ), BF16),
             pltpu.VMEM((D, SEQ), BF16),
-            pltpu.VMEM((D, SEQ), F32),
+            pltpu.VMEM((D, SEQ), BF16),
             pltpu.VMEM((1, SEQ), F32),
             pltpu.VMEM((3 * D, SEQ), BF16),
             pltpu.VMEM((3 * D, SEQ), BF16),
             pltpu.VMEM((D, SEQ), BF16),
             pltpu.VMEM((D, SEQ), BF16),
+            pltpu.VMEM((D, SEQ), F32),
+            pltpu.VMEM((D, SEQ), F32),
             pltpu.VMEM((1, SEQ), F32),
             pltpu.VMEM((NCKPT, 1, SEQ), F32),
-            pltpu.SemaphoreType.DMA((4,)),
+            pltpu.SemaphoreType.DMA((5,)),
             pltpu.SemaphoreType.DMA((4,)),
             pltpu.SemaphoreType.DMA((2, 2, 4, 3)),
             pltpu.SemaphoreType.DMA((2, 9)),
-            pltpu.SemaphoreType.DMA((NZ + 1,)),
+            pltpu.SemaphoreType.DMA((2, NZ)),
             pltpu.SemaphoreType.DMA((NCKPT,)),
         ],
         compiler_params=pltpu.CompilerParams(

time: 57.3 us -> 56.7 us (0.990)
  Pallas kernels: 55.9 us -> 55.3 us
    pallas_call x1, Pallas kernels: 55.9 us -> 55.3 us  [per_device(): pl.pallas_call(kernel, out_shape=jax.ShapeDtypeStruct((1, SEQ), F32), in_...]
where the time goes in v5:
time: 56.7 us; the launch traced here: 56.6 us
  Pallas kernels  55.3 us (98%)
  local copies, waits for them, and re-layouts  1.26 us (2%)
    pallas_call x1, Pallas kernels, per_device(): pl.pallas_call(kernel, out_shape=jax.ShapeDtypeStruct((1, SEQ), F32), in_...  55.3 us
    unnamed x1, local copies, waits for them, and re-layouts  1.26 us

profile of v5, /device:TPU:1, one launch (start us, length us, event | category | flops | bytes accessed | tf_op | source)
XLA Modules:
  0.0 56.6 jit_solution(449135298807756235)
XLA Ops:
  0.0 55.3 %scores.1 = f32[1,512]{1,0:T(1,128)} custom-call(bf16[1,512,768]{2,1,0:T(8,128)(2,1)} %x_hbm.1, bf16[1,512,768]{2,1,0:T(8,128)(2,1)} %t_hbm.1, bf16[1,512,768]{2,1,0:T(8,128)(2,1)} %g_hbm.1, bf16[1,768]{1,0:T(2,128)(2,1)} %gain_hbm.1, bf16[1,768]{1,0:T(2,128)(2,1)} %cost_hbm.1, bf16[1,72,768]{2,1,0:T(8,128)(2,1)} %wq_hbm.1, bf16[1,72,768]{2,1,0:T(8,128)(2,1)} %cq_hbm.1, ...), custom_call_target="tpu_custom_call" | custom-call | flops 8999999488 | bytes 3000000 | tf_op jit(solution)/shard_map/scores/pallas_call | solution.py:364
  55.3 1.3 %copy.11 = f32[512]{0:T(512)} copy(f32[512]{0:T(512)} %bitcast.1) | data formatting | bytes 4096

commit v6 on v5

--- a/solution.py
+++ b/solution.py
@@ -170,7 +170,7 @@
     x_ref, t_ref, g_ref, gain_ref, cost_ref, wq_ref, cq_ref, wo_ref, co_ref,
     gq_ref, go_ref, lt_ref, ltt_ref, gt_ref, res_ref, p_ref, dp_ref, at_ref, dat_ref, u_ref, uc_ref,
     mine_ref, sums_ref,
-    in_sem, sent, ring_r, y_r, twin_r, sum_r,
+    in_sem, sent, ring_r, y_r, twin_r, sum_s, sum_r,
 ):
     ck = lax.axis_index("ckpt")
     me = lax.axis_index("fsdp")
@@ -193,7 +193,7 @@
     for peer in (up, down, side, twin):
         pl.semaphore_signal(barrier, inc=1, device_id={"fsdp": peer}, device_id_type=MESH)
     for i, src, dst in (
-        (0, wq_hbm.at[0], wq_ref), (0, cq_hbm.at[0], cq_ref), (4, wo_hbm.at[0], wo_ref), (4, co_hbm.at[0], co_ref),
+        (0, wq_hbm.at[0], wq_ref), (5, cq_hbm.at[0], cq_ref), (4, wo_hbm.at[0], wo_ref), (6, co_hbm.at[0], co_ref),
     ):
         pltpu.make_async_copy(src, dst, in_sem.at[i]).start()
     for k in range(1, NCKPT):
@@ -266,7 +266,8 @@
 
     def begin(ph):
         if ph == 1:
-            landed(go_ref.at[0], in_sem.at[4], ("in", 0))
+            landed(wo_ref, in_sem.at[4], ("in", 0))
+            landed(co_ref, in_sem.at[6], ("in", 0))
             go_ref[me] = jnp.concatenate([wo_ref[...].astype(F32), co_ref[...].astype(F32)], axis=0).astype(BF16)
         y_send(ph, 1, 0)
         for pi in (0, 1):
@@ -338,7 +339,8 @@
         elif kind == "N":
             load_rest()
 
-    landed(gq_ref.at[0], in_sem.at[0], ("in", 0))
+    landed(wq_ref, in_sem.at[0], ("in", 0))
+    landed(cq_ref, in_sem.at[5], ("in", 0))
     gq_ref[me] = jnp.concatenate([wq_ref[...].astype(F32), cq_ref[...].astype(F32)], axis=0).astype(BF16)
     pl.semaphore_wait(barrier, 4 + NCKPT - 1)
     for op in ORDER:
@@ -346,7 +348,7 @@
     mine_ref[...] = out_scores(at_ref, dat_ref, u_ref, uc_ref) + res_ref[...]
 
     for k in range(1, NCKPT):
-        remote(mine_ref, sums_ref.at[k], sent.at[3], sum_r.at[k], {"ckpt": (ck + k) % NCKPT}, ("sum", 0, k))
+        remote(mine_ref, sums_ref.at[k], sum_s.at[k], sum_r.at[k], {"ckpt": (ck + k) % NCKPT}, ("sum", 0, k))
     landed(gq_ref.at[pl.ds(0, 20)], sent.at[0], ("sent", 0))
     landed(gq_ref.at[pl.ds(0, 16)], sent.at[1], ("sent", 1))
     landed(go_ref.at[pl.ds(0, 16)], sent.at[2], ("sent", 2))
@@ -355,7 +357,8 @@
         landed(sums_ref.at[k], sum_r.at[k], ("sum", 0, k))
         total = total + sums_ref[k]
     out_ref[...] = total
-    landed(sums_ref.at[pl.ds(1, NCKPT - 1)], sent.at[3], ("sent", 3))
+    for k in range(1, NCKPT):
+        landed(mine_ref, sum_s.at[k], ("sent", 3))
 
 
 def per_device(states, state_tangent, loss_grad, norm_gain, gain_costate, qkv_weight, qkv_costate, out_weight, out_costate):
@@ -390,11 +393,12 @@
             pltpu.VMEM((D, SEQ), F32),
             pltpu.VMEM((1, SEQ), F32),
             pltpu.VMEM((NCKPT, 1, SEQ), F32),
-            pltpu.SemaphoreType.DMA((5,)),
-            pltpu.SemaphoreType.DMA((4,)),
+            pltpu.SemaphoreType.DMA((7,)),
+            pltpu.SemaphoreType.DMA((3,)),
             pltpu.SemaphoreType.DMA((2, 2, 4, 3)),
             pltpu.SemaphoreType.DMA((2, 9)),
             pltpu.SemaphoreType.DMA((2, NZ)),
+            pltpu.SemaphoreType.DMA((NCKPT,)),
             pltpu.SemaphoreType.DMA((NCKPT,)),
         ],
         compiler_params=pltpu.CompilerParams(

time: 56.7 us -> 56.8 us (level)
  no operation moved by 1% of the time
where the time goes in v6:
time: 56.8 us; the launch traced here: 56.6 us
  Pallas kernels  55.4 us (98%)
  local copies, waits for them, and re-layouts  1.26 us (2%)
    pallas_call x1, Pallas kernels, per_device(): pl.pallas_call(kernel, out_shape=jax.ShapeDtypeStruct((1, SEQ), F32), in_...  55.4 us
    unnamed x1, local copies, waits for them, and re-layouts  1.26 us

profile of v6, /device:TPU:1, one launch (start us, length us, event | category | flops | bytes accessed | tf_op | source)
XLA Modules:
  0.0 56.6 jit_solution(11632051782842336993)
XLA Ops:
  0.0 55.4 %scores.1 = f32[1,512]{1,0:T(1,128)} custom-call(bf16[1,512,768]{2,1,0:T(8,128)(2,1)} %x_hbm.1, bf16[1,512,768]{2,1,0:T(8,128)(2,1)} %t_hbm.1, bf16[1,512,768]{2,1,0:T(8,128)(2,1)} %g_hbm.1, bf16[1,768]{1,0:T(2,128)(2,1)} %gain_hbm.1, bf16[1,768]{1,0:T(2,128)(2,1)} %cost_hbm.1, bf16[1,72,768]{2,1,0:T(8,128)(2,1)} %wq_hbm.1, bf16[1,72,768]{2,1,0:T(8,128)(2,1)} %cq_hbm.1, ...), custom_call_target="tpu_custom_call" | custom-call | flops 8999999488 | bytes 3000000 | tf_op jit(solution)/shard_map/scores/pallas_call | solution.py:367
  55.4 1.3 %copy.11 = f32[512]{0:T(512)} copy(f32[512]{0:T(512)} %bitcast.1) | data formatting | bytes 4096
